TPU v7x, 32 devices: a whole 2x2x4 slice. The times are simulated.
32 devices in a mesh: row: 4 (over y, x), tile: 8 (over z, core).
Axes of the slice: x: 2, y: 2, z: 4, core: 2. Of those that a mesh axis runs over, the one named last changes fastest.
Arguments:
- row_points: float32 [3, 16384], replicated, may hold values from 0 to 6, as said below
- source_points: float32 [3, 32768], P(None, 'tile'), may hold values from -2.5 to 6, as said below
- sketch: bfloat16 [32768, 128], P('tile'), may hold values from -6 to 6
- admissible: int32 [4, 256], P('row', 'tile'), may hold values from 0 to 1, as said below
Outputs:
- basis: float32 [16384, 128], P(('row', 'tile'))
- projected: bfloat16 [4, 128, 32768], P('row', None, 'tile')
Inputs may be any that keep to these rules, and one draw needn't show every extreme that they name: In every block row, the 32 panels of some index of tile are all admissible; how many panels of an index of tile are admissible varies widely. `row_points`: the first two coordinates lie in 0 to 6 and the third in 0 to 0.25. `source_points`: the first two coordinates lie in 0 to 6 and the third in -2.5 to -0.5.
All inputs are finite; a program needn't handle non-finite values.
Results may differ from a plain program's by a relative error of at most 0.0055.
Values may be sent and summed in bfloat16 or wider, within the bound.
No kernel may reach another device: no remote copies, remote signals or barrier semaphores. Data moves between devices by JAX's collectives and lax.ppermute only.
A program may use at most 64 MiB of HBM per device.

v0:
```python
import functools
import math

import jax
import jax.numpy as jnp
from jax import lax
from jax.experimental import pallas as pl
from jax.experimental.pallas import tpu as pltpu
from jax.sharding import PartitionSpec as P

DAMPING = 0.25
WAVENUM = 24.0
SHIFT = 0.0001

TURNS = WAVENUM / (2.0 * math.pi)
DECAY = -DAMPING / TURNS / math.log(2.0)
AMP = TURNS / (4.0 * math.pi)
S0, S1, S2 = 6.28127979 * AMP, -41.0952178 * AMP, 73.5851113 * AMP

WIDTH = 128
PAIR = 2 * WIDTH
TERMS = 32
SUB = 8
PIECE = 16
GROUP = 8
FEW = 4
HALF = FEW * WIDTH
WHOLE = 1.5 * 2.0**23


def head(x):
    return x.astype(jnp.bfloat16).astype(jnp.float32)


def three(x):
    a = head(x)
    b = head(x - a)
    return a, b, x - a - b


def fill_terms(ref, points, side):
    at = lax.broadcasted_iota(jnp.int32, points.shape, 0)
    x = points - jnp.where(at == 2, -0.5, 3.0)
    scale = TURNS * TURNS
    norm = three(scale * jnp.sum(x * x, axis=0, keepdims=True))
    one = jnp.ones_like(norm[0])
    if side == 0:
        h, m, l = three(x)
        rows = [h, h, m, h, l, m]
        tail = [*norm, one, one, one]
    else:
        h, m, l = three(x * (-2.0 * scale))
        rows = [h, m, h, l, h, m]
        tail = [one, one, one, *norm]
    ref[...] = jnp.zeros_like(ref)
    for at, row in enumerate(rows):
        ref[3 * at : 3 * at + 3, :] = row
    for at, row in enumerate(tail):
        ref[18 + at : 19 + at, :] = row


def near_field(square):
    inv = lax.rsqrt(square)
    t = square * inv
    f = t - ((t + WHOLE) - WHOLE)
    g = 0.25 - jnp.abs(f)
    v = g * g
    wave = ((S2 * v + S1) * v + S0) * g
    amp = jnp.exp2(DECAY * t) * inv
    return (wave * amp).astype(jnp.bfloat16)


def order_panels(flags_ref, order_ref, panels):
    def step(p, count):
        @pl.when(flags_ref[0, p] > 0)
        def _():
            order_ref[count] = p

        return count + (flags_ref[0, p] > 0).astype(jnp.int32)

    count = lax.fori_loop(0, panels, step, jnp.int32(0))
    order_ref[panels] = count
    return count


def prep_kernel(
    flags_hbm, rows_hbm, src_hbm, omega_hbm, order_ref, src_pick, omega_pick, row_mat,
    flags, points, picked, row_terms, src_terms, sources, sems, sem, *, slices, place
):
    panels = flags.shape[1]
    rows = points.shape[1]
    me = lax.axis_index("tile")
    at = pl.multiple_of(lax.axis_index("row") * rows, rows) if place else 0
    copies = [
        pltpu.make_async_copy(flags_hbm, flags, sems.at[0]),
        pltpu.make_async_copy(rows_hbm.at[:, pl.ds(at, rows)], points, sems.at[1]),
        pltpu.make_async_copy(src_hbm, sources, sems.at[2]),
    ]
    for copy in copies:
        copy.start()
    copies[0].wait()
    count = order_panels(flags, order_ref, panels)

    def fetch(slot):
        at = pl.multiple_of(order_ref[slot] * WIDTH, WIDTH)
        to = pl.multiple_of(slot * WIDTH, WIDTH)
        return pltpu.make_async_copy(
            omega_hbm.at[pl.ds(at, WIDTH), :], omega_pick.at[pl.ds(to, WIDTH), :], sem
        )

    def start(slot, carry):
        fetch(slot).start()
        return carry

    lax.fori_loop(0, count, start, 0)
    copies[1].wait()
    if place:
        to = 0
        for k, first, size in slices:
            at = pl.multiple_of((me ^ k) * (rows // lax.axis_size("tile")) + first, WIDTH)
            picked[:, to : to + size] = points[:, pl.ds(at, size)]
            to += size
        fill_terms(row_terms, picked[...], 0)
    else:
        fill_terms(row_terms, points[...], 0)
    step = min(512, rows)
    for r in range(0, rows, step):
        row_mat[r : r + step, :] = row_terms[:, r : r + step].T.astype(jnp.bfloat16)
    copies[2].wait()
    fill_terms(src_terms, sources[...], 1)

    def pick(slot, carry):
        at = pl.multiple_of(order_ref[slot] * WIDTH, WIDTH)
        to = pl.multiple_of(slot * WIDTH, WIDTH)
        src_pick[:, pl.ds(to, WIDTH)] = src_terms[:, pl.ds(at, WIDTH)].astype(jnp.bfloat16)
        return carry

    lax.fori_loop(0, count, pick, 0)
    spare = src_terms[:, :WIDTH].astype(jnp.bfloat16)

    def pad(slot, carry):
        to = pl.multiple_of(slot * WIDTH, WIDTH)
        src_pick[:, pl.ds(to, WIDTH)] = spare
        omega_pick[pl.ds(to, WIDTH), :] = jnp.zeros((WIDTH, omega_pick.shape[1]), jnp.bfloat16)
        return carry

    lax.fori_loop(count, GROUP * ((count + GROUP - 1) // GROUP), pad, 0)

    def finish(slot, carry):
        fetch(slot).wait()
        return carry

    lax.fori_loop(0, count, finish, 0)


def in_hbm(x):
    return pltpu.with_memory_space_constraint(x, pltpu.HBM)


def prep(admissible, points, source_points, sketch, rows, slices, place):
    panels = admissible.shape[1]
    cols, rank = sketch.shape
    spare = GROUP * ((panels + GROUP - 1) // GROUP) * WIDTH
    hbm = pl.BlockSpec(memory_space=pltpu.HBM)
    vmem = pl.BlockSpec(memory_space=pltpu.VMEM)
    return pl.pallas_call(
        functools.partial(prep_kernel, slices=slices, place=place),
        in_specs=[hbm] * 4,
        out_specs=[pl.BlockSpec(memory_space=pltpu.SMEM), vmem, vmem, vmem],
        out_shape=[
            jax.ShapeDtypeStruct((panels + 8,), jnp.int32),
            jax.ShapeDtypeStruct((TERMS, spare), jnp.bfloat16),
            jax.ShapeDtypeStruct((spare, rank), jnp.bfloat16),
            jax.ShapeDtypeStruct((rows, TERMS), jnp.bfloat16),
        ],
        scratch_shapes=[
            pltpu.SMEM((1, panels), jnp.int32),
            pltpu.VMEM((3, rows), jnp.float32),
            pltpu.VMEM((3, rows), jnp.float32),
            pltpu.VMEM((TERMS, rows), jnp.float32),
            pltpu.VMEM((TERMS, cols), jnp.float32),
            pltpu.VMEM((3, cols), jnp.float32),
            pltpu.SemaphoreType.DMA((3,)),
            pltpu.SemaphoreType.DMA,
        ],
        compiler_params=pltpu.CompilerParams(vmem_limit_bytes=16 * 2**20),
        name="prep",
    )(*(in_hbm(x) for x in (admissible, points, source_points, sketch)))


def sketch_kernel(
    order_ref, src_pick, omega_pick, row_mat, part_ref, tiles_ref, total, *, first, panels, rb
):
    groups = (order_ref[panels] + GROUP - 1) // GROUP
    cols = GROUP * WIDTH

    def block(b, carry):
        here = pl.ds(pl.multiple_of(b * rb, rb), rb)
        total[...] = jnp.zeros_like(total)

        def body(j, carry):
            at = pl.ds(pl.multiple_of(j * cols, cols), cols)
            rows = row_mat[pl.ds(pl.multiple_of(first + b * rb, rb), rb), :]
            src = src_pick[:, at]
            omega = omega_pick[at, :]
            sums = total[...]
            near = []
            for c in range(0, cols, HALF):
                square = jnp.dot(rows, src[:, c : c + HALF], preferred_element_type=jnp.float32)
                tile = [near_field(square[r : r + PIECE]) for r in range(0, rb, PIECE)]
                tile = jnp.concatenate(tile, axis=0)
                sums += jnp.dot(tile, omega[c : c + HALF], preferred_element_type=jnp.float32)
                near.append(tile)
            total[...] = sums
            for k in range(GROUP):
                tile = near[k * WIDTH // HALF]
                at = k * WIDTH % HALF
                tiles_ref[GROUP * j + k, here, :] = tile[:, at : at + WIDTH]
            return carry

        lax.fori_loop(0, groups, body, 0)
        part_ref[here, :] = total[...]
        return carry

    lax.fori_loop(0, part_ref.shape[0] // rb, block, 0)


def sketch_pass(order, src_pick, omega_pick, row_mat, first, rows, panels):
    rank = omega_pick.shape[1]
    rb = min(512, rows)
    vmem = pl.BlockSpec(memory_space=pltpu.VMEM)
    return pl.pallas_call(
        functools.partial(sketch_kernel, first=first, panels=panels, rb=rb),
        in_specs=[pl.BlockSpec(memory_space=pltpu.SMEM), vmem, vmem, vmem],
        out_specs=[vmem, vmem],
        out_shape=[
            jax.ShapeDtypeStruct((rows, rank), jnp.float32),
            pltpu.VMEM((GROUP * ((panels + GROUP - 1) // GROUP), rows, WIDTH), jnp.bfloat16),
        ],
        scratch_shapes=[
            pltpu.VMEM((rb, rank), jnp.float32),
        ],
        compiler_params=pltpu.CompilerParams(vmem_limit_bytes=10 * 2**20),
        cost_estimate=pl.CostEstimate(
            flops=rows * panels * WIDTH * rank * 16, bytes_accessed=rows * panels * WIDTH * 2, transcendentals=0
        ),
        name="sketch_pass",
    )(order, src_pick, omega_pick, row_mat)


def in_vmem(kernel, out_shape, name):
    def call(*args):
        vmem = pl.BlockSpec(memory_space=pltpu.VMEM)
        return pl.pallas_call(
            kernel,
            in_specs=[vmem] * len(args),
            out_specs=jax.tree.map(lambda _: vmem, out_shape),
            out_shape=out_shape,
            compiler_params=pltpu.CompilerParams(vmem_limit_bytes=8 * 2**20),
            name=name,
        )(*args)

    return call


def pair_sum_kernel(own_ref, got_ref, kept_ref, *sent_refs):
    q = kept_ref.shape[0]
    for k in range(1 + len(sent_refs)):
        part = slice(k * q, (k + 1) * q)
        value = own_ref[part, :] + got_ref[part, :]
        if k == 0:
            kept_ref[...] = value
        else:
            sent_refs[k - 1][...] = value.astype(jnp.bfloat16)


def pair_sum(own, got, slots):
    q, rank = own.shape[0] // slots, own.shape[1]
    shapes = [jax.ShapeDtypeStruct((q, rank), jnp.float32)]
    shapes += [jax.ShapeDtypeStruct((q, rank), jnp.bfloat16)] * (slots - 1)
    return in_vmem(pair_sum_kernel, shapes, "pair_sum")(own, got)


def row_sum_kernel(kept_ref, *refs):
    total = kept_ref[...]
    for ref in refs[:-1]:
        total = total + ref[...].astype(jnp.float32)
    low = head(total)
    refs[-1][...] = (low if refs[-1].shape == low.shape else low.T).astype(jnp.bfloat16)


def row_sum(kept, got, flip):
    shape = kept.shape[::-1] if flip else kept.shape
    return in_vmem(row_sum_kernel, jax.ShapeDtypeStruct(shape, jnp.bfloat16), "row_sum")(kept, *got)


def invert_factor(gram, beside):
    n = gram.shape[0]
    pieces = n // SUB
    lane = lax.broadcasted_iota(jnp.int32, (SUB, n), 1)
    sub = lax.broadcasted_iota(jnp.int32, (SUB, n), 0)
    trace = jnp.zeros((SUB, n), jnp.float32)
    for v in range(pieces):
        trace = trace + jnp.where(lane == sub + v * SUB, gram[v * SUB : (v + 1) * SUB, :], 0.0)
    shift = (SHIFT / n) * jnp.sum(trace)
    a = [
        gram[v * SUB : (v + 1) * SUB, :] + jnp.where(lane == sub + v * SUB, shift, 0.0)
        for v in range(pieces)
    ]
    for b in range(pieces):
        beside(b)
        cols = [
            {v: jnp.broadcast_to(a[v][:, b * SUB + c : b * SUB + c + 1], (SUB, n)) for v in range(b, pieces)}
            for c in range(SUB)
        ]
        for c in range(SUB):
            j = b * SUB + c
            pivot = jnp.broadcast_to(cols[c][b][c : c + 1, :], (SUB, n))
            inv = 1.0 / pivot
            row = jnp.broadcast_to(a[b][c : c + 1, :], (SUB, n))
            row = jnp.where(lane == j, 1.0, row)
            nexts = {
                c2: jnp.broadcast_to(cols[c2][b][c : c + 1, :], (SUB, n)) for c2 in range(c + 1, SUB)
            }
            for v in range(b, pieces):
                m = cols[c][v] * inv
                here = lane == j
                if v == b:
                    m = jnp.where(sub > c, m, 0.0)
                    here = here & (sub > c)
                a[v] = jnp.where(here, 0.0, a[v]) - m * row
                for c2 in range(c + 1, SUB):
                    cols[c2][v] = cols[c2][v] - m * nexts[c2]
    out = []
    for v in range(pieces):
        diag = lane == sub + v * SUB
        d = jnp.sum(jnp.where(diag, a[v], 0.0), axis=1, keepdims=True)
        low = jnp.where(lane < sub + v * SUB, a[v], jnp.where(diag, 1.0, 0.0))
        out.append(low * lax.rsqrt(d))
    return jnp.concatenate(out, axis=0)


def gather_low(odd_ref, even_refs, low_all, flip):
    half, q = odd_ref.shape[0], odd_ref.shape[2 if flip else 1]
    pieces = [odd_ref.at[k] for k in range(half)] + list(even_refs)
    for i, ref in enumerate(pieces):
        if flip:
            low_all[:, i * q : (i + 1) * q] = ref[...]
        else:
            low_all[i * q : (i + 1) * q, :] = ref[...]
    return low_all[...] if flip else low_all[...].T


def self_product(low_t):
    return lax.dot_general(low_t, low_t, (((1,), (1,)), ((), ())), preferred_element_type=jnp.float32)


def side_by_side(tile_refs, first, count):
    return jnp.concatenate(
        [jnp.concatenate([ref[first + k] for k in range(count)], axis=1) for ref in tile_refs], axis=0
    )


def first_kernel(order_ref, odd_ref, *refs, panels, half, flip):
    even_refs, tile_refs = refs[:half], refs[half:-3]
    product_ref, gram_ref, low_all = refs[-3:]
    low_t = gather_low(odd_ref, even_refs, low_all, flip)
    gram_ref[...] = self_product(low_t)

    def group(j, carry):
        at = pl.ds(pl.multiple_of(j * HALF, HALF), HALF)
        product_ref[:, at] = jnp.dot(
            low_t, side_by_side(tile_refs, FEW * j, FEW), preferred_element_type=jnp.float32
        )
        return carry

    lax.fori_loop(0, (order_ref[panels] + FEW - 1) // FEW, group, 0)


def first_pass(order, odd, even, tiles, panels, rank, flip):
    rows = sum(t.shape[1] for t in tiles)
    held = tiles[0].shape[0]
    vmem = pl.BlockSpec(memory_space=pltpu.VMEM)
    return pl.pallas_call(
        functools.partial(first_kernel, panels=panels, half=len(even), flip=flip),
        in_specs=[pl.BlockSpec(memory_space=pltpu.SMEM)] + [vmem] * (1 + len(even) + len(tiles)),
        out_specs=[vmem, vmem],
        out_shape=[
            jax.ShapeDtypeStruct((rank, held * WIDTH), jnp.float32),
            jax.ShapeDtypeStruct((rank, rank), jnp.float32),
        ],
        scratch_shapes=[pltpu.VMEM((rank, rows) if flip else (rows, rank), jnp.bfloat16)],
        compiler_params=pltpu.CompilerParams(vmem_limit_bytes=12 * 2**20),
        cost_estimate=pl.CostEstimate(
            flops=2 * rows * panels * WIDTH * rank, bytes_accessed=0, transcendentals=0
        ),
        name="first_pass",
    )(order, odd, *even, *(pltpu.with_memory_space_constraint(x, pltpu.VMEM) for x in tiles))


def project_kernel(order_ref, first_ref, gram_ref, odd_ref, *refs, panels, half, owns, flip):
    own_refs, even_refs = refs[:owns], refs[owns : owns + half]
    tile_refs = refs[owns + half : -4]
    basis_ref, out_ref, low_all, product = refs[-4:]
    count = order_ref[panels]
    low_t = gather_low(odd_ref, even_refs, low_all, flip)
    out_ref[...] = jnp.zeros_like(out_ref)
    pairs = tile_refs[0].shape[0] // 2
    blocks = gram_ref.shape[0] // SUB

    def beside(b):
        for j in range(b * pairs // blocks, (b + 1) * pairs // blocks):
            at = slice(j * PAIR, (j + 1) * PAIR)
            product[:, at] = first_ref[:, at] + jnp.dot(
                low_t, side_by_side(tile_refs, 2 * j, 2), preferred_element_type=jnp.float32
            )

    inverse = three(invert_factor(gram_ref[...] + self_product(low_t), beside))
    rank = inverse[0].shape[0]
    stack = jnp.concatenate(inverse, axis=0).astype(jnp.bfloat16)
    q = own_refs[0].shape[1 if flip else 0]
    for i, ref in enumerate(own_refs):
        own = ref[...] if flip else ref[...].T
        parts = jnp.dot(stack, own, preferred_element_type=jnp.float32)
        basis = parts[:rank] + (parts[rank : 2 * rank] + parts[2 * rank :])
        basis_ref[i * q : (i + 1) * q, :] = basis.T

    def group(j, carry):
        parts = three(product[:, pl.ds(pl.multiple_of(j * HALF, HALF), HALF)])
        cols, rest = 0.0, 0.0
        for k, part in enumerate(parts):
            got = jnp.dot(
                stack[: (3 - k) * rank], part.astype(jnp.bfloat16), preferred_element_type=jnp.float32
            )
            for i in range(3 - k):
                if i + k == 0:
                    cols = got[:rank]
                else:
                    rest = rest + got[i * rank : (i + 1) * rank]
        cols = (cols + rest).astype(jnp.bfloat16)
        for k in range(FEW):

            @pl.when(FEW * j + k < count)
            def _():
                at = pl.multiple_of(order_ref[FEW * j + k] * WIDTH, WIDTH)
                out_ref[0, :, pl.ds(at, WIDTH)] = cols[:, k * WIDTH : (k + 1) * WIDTH]

        return carry

    lax.fori_loop(0, (count + FEW - 1) // FEW, group, 0)


def project_pass(order, first, gram, odd, owns, even, tiles, panels, rank, flip):
    rows = sum(t.shape[1] for t in tiles)
    held = tiles[0].shape[0]
    q = owns[0].shape[1 if flip else 0]
    vmem = pl.BlockSpec(memory_space=pltpu.VMEM)
    return pl.pallas_call(
        functools.partial(
            project_kernel, panels=panels, half=len(even), owns=len(owns), flip=flip
        ),
        in_specs=[pl.BlockSpec(memory_space=pltpu.SMEM)]
        + [vmem] * (3 + len(owns) + len(even) + len(tiles)),
        out_specs=[vmem, vmem],
        out_shape=[
            jax.ShapeDtypeStruct((q * len(owns), rank), jnp.float32),
            jax.ShapeDtypeStruct((1, rank, panels * WIDTH), jnp.bfloat16),
        ],
        scratch_shapes=[
            pltpu.VMEM((rank, rows) if flip else (rows, rank), jnp.bfloat16),
            pltpu.VMEM((rank, held * WIDTH), jnp.float32),
        ],
        compiler_params=pltpu.CompilerParams(vmem_limit_bytes=14 * 2**20),
        name="project_pass",
    )(
        order, first, gram, odd, *owns, *even,
        *(pltpu.with_memory_space_constraint(x, pltpu.VMEM) for x in tiles),
    )


def join_kernel(*refs):
    for k, ref in enumerate(refs[:-1]):
        refs[-1][k] = ref[...]


def join(parts):
    shape = jax.ShapeDtypeStruct((len(parts), *parts[0].shape), parts[0].dtype)
    return in_vmem(join_kernel, shape, "join")(*parts)


def after(x, *deps):
    return lax.optimization_barrier((x, *deps))[0]


def swap(x, k, n):
    return lax.ppermute(x, "tile", [(i, i ^ k) for i in range(n)])


CHUNKS = 2


def local(row_points, source_points, sketch, admissible):
    n = lax.axis_size("tile")
    panels = admissible.shape[1]
    rows = row_points.shape[1] // lax.axis_size("row")
    own_rows = rows // n
    q = own_rows // CHUNKS
    odd, even = list(range(1, n, 2)), list(range(0, n, 2))
    slices = [(k, c * q, q) for c in range(CHUNKS) for k in odd + even]
    place = flip = q % WIDTH == 0
    points = row_points
    if not place:
        me = lax.axis_index("tile")
        points = lax.dynamic_slice_in_dim(row_points, lax.axis_index("row") * rows, rows, 1)
        points = jnp.concatenate(
            [lax.dynamic_slice_in_dim(points, (me ^ k) * own_rows + first, q, 1) for k, first, _ in slices], 1
        )
    order, src_pick, omega_pick, row_mat = prep(
        admissible, points, source_points, sketch, rows, slices, place
    )

    call_rows = rows // CHUNKS // 2

    def sketch_part(at, *deps):
        return sketch_pass(
            after(order, *deps), src_pick, omega_pick, row_mat, at * call_rows, call_rows, panels
        )

    def sum_cores(got, own):
        kept, *sent = pair_sum(own, got, n // 2)
        return kept, [swap(x, k, n) for x, k in zip(sent, even[1:])]

    def along_z(kept, got):
        low = row_sum(kept, got, flip)
        return [low] + [swap(low, k, n) for k in even[1:]]

    held, tiles, sums, last = [], [], None, ()
    for c in range(CHUNKS):
        theirs, kept = sketch_part(2 * c, *last)
        tiles.append(kept)
        got = swap(theirs, 1, n)
        if c > 0:
            held.append(along_z(after(sums[0], theirs), sums[1]))
        own, kept = sketch_part(2 * c + 1, theirs, *[h[0] for h in held[-1:]])
        tiles.append(kept)
        sums = sum_cores(got, after(own, *(x for h in held[-1:] for x in h)))
        last = (own, sums[0])
    held.append(along_z(*sums))
    rank = sketch.shape[1]
    odds = [swap(join([after(h[0], own), *h[1:]]), 1, n) for h in held]
    first, gram = first_pass(order, odds[0], held[0], tiles[:2], panels, rank, flip)
    owns = [h[0] for h in held]
    return project_pass(
        order, first, gram, odds[1], owns, held[1], tiles[2:], panels, rank, flip
    )


def solution(mesh):
    in_specs = (P(), P(None, "tile"), P("tile", None), P("row", "tile"))
    out_specs = (P(("row", "tile"), None), P("row", None, "tile"))
    return jax.shard_map(local, mesh=mesh, in_specs=in_specs, out_specs=out_specs, check_vma=False)
```

profile of v0, /device:TPU:0, one launch (start us, length us, event | category | flops | bytes accessed | tf_op | source)
XLA Modules:
  0.0 100.5 jit_solution(5684941512837001951)
XLA Ops:
  0.6 2.9 %prep.1 = (s32[40]{0:T(128)S(1)}, bf16[32,4096]{1,0:T(8,128)(2,1)S(1)}, bf16[4096,128]{1,0:T(8,128)(2,1)S(1)}, bf16[4096,32]{1,0:T(8,128)(2,1)S(1)}) custom-call(s32[1,32]{1,0:T(1,128)} %flags_hbm.1, f32[3,16384]{1,0:T(4,128)} %rows_hbm.1, f32[3,4096]{1,0:T(4,128)} %src_hbm.1, bf16[4096,128]{1,0:T(8,128)(2,1)} %omega_hbm.1), custom_call_target="tpu_custom_call" | custom-call | tf_op jit(solution)/shard_map/prep/pallas_call | solution.py:166
  3.6 13.9 %sketch_pass.4 = (f32[1024,128]{1,0:T(8,128)S(1)}, bf16[32,1024,128]{2,1,0:T(8,128)(2,1)S(1)}) custom-call(s32[40]{0:T(128)S(1)} %get-tuple-element.45.order_ref, bf16[32,4096]{1,0:T(8,128)(2,1)S(1)} %get-tuple-element.32.src_pick, bf16[4096,128]{1,0:T(8,128)(2,1)S(1)} %get-tuple-element.33.omega_pick, bf16[4096,32]{1,0:T(8,128)(2,1)S(1)} %get-tuple-element.34.row_mat), custom_call_target="tpu_custom_call" | custom-call | flops 8589934592 | bytes 8388608 | tf_op jit(solution)/shard_map/sketch_pass/pallas_call | solution.py:232
  17.4 0.1 collective-permute-start
  17.5 13.9 %sketch_pass.5 = (f32[1024,128]{1,0:T(8,128)S(1)}, bf16[32,1024,128]{2,1,0:T(8,128)(2,1)S(1)}) custom-call(s32[40]{0:T(128)S(1)} %get-tuple-element.45.order_ref, bf16[32,4096]{1,0:T(8,128)(2,1)S(1)} %get-tuple-element.32.src_pick, bf16[4096,128]{1,0:T(8,128)(2,1)S(1)} %get-tuple-element.33.omega_pick, bf16[4096,32]{1,0:T(8,128)(2,1)S(1)} %get-tuple-element.34.row_mat), custom_call_target="tpu_custom_call" | custom-call | flops 8589934592 | bytes 8388608 | tf_op jit(solution)/shard_map/sketch_pass/pallas_call | solution.py:232
  31.4 0.0 collective-permute-done.got_ref
  31.4 0.1 pair_sum.2
  31.5 0.1 collective-permute-start.1
  31.6 0.1 collective-permute-start.2
  31.7 4.3 %collective-permute-start.3 = (bf16[256,128]{1,0:T(8,128)(2,1)S(1)}, bf16[256,128]{1,0:T(8,128)(2,1)S(1)}, u32[]{:S(2)}, u32[]{:S(2)}) collective-permute-start(bf16[256,128]{1,0:T(8,128)(2,1)S(1)} %get-tuple-element.44), channel_id=1, source_target_pairs={{0,6},{1,7},{2,4},{3,5},{4,2},{5,3},{6,0},{7,1},{8,14},{9,15},{10,... | collective-permute-start | bytes 196616 | tf_op jit(solution)/shard_map/ppermute | solution.py:496
  35.9 13.9 %sketch_pass.6 = (f32[1024,128]{1,0:T(8,128)S(1)}, bf16[32,1024,128]{2,1,0:T(8,128)(2,1)S(1)}) custom-call(s32[40]{0:T(128)S(1)} %get-tuple-element.45.order_ref, bf16[32,4096]{1,0:T(8,128)(2,1)S(1)} %get-tuple-element.32.src_pick, bf16[4096,128]{1,0:T(8,128)(2,1)S(1)} %get-tuple-element.33.omega_pick, bf16[4096,32]{1,0:T(8,128)(2,1)S(1)} %get-tuple-element.34.row_mat), custom_call_target="tpu_custom_call" | custom-call | flops 8589934592 | bytes 8388608 | tf_op jit(solution)/shard_map/sketch_pass/pallas_call | solution.py:232
  49.8 0.1 collective-permute-start.8
  49.9 0.0 collective-permute-done.1.refs_0_
  49.9 0.0 collective-permute-done.2.refs_1_
  49.9 0.0 collective-permute-done.3.refs_2_
  50.0 0.1 row_sum.2.refs_0_
  50.1 0.1 collective-permute-start.4
  50.1 0.1 collective-permute-start.5
  50.2 4.3 %collective-permute-start.6 = (bf16[128,256]{1,0:T(8,128)(2,1)S(1)}, bf16[128,256]{1,0:T(8,128)(2,1)S(1)}, u32[]{:S(2)}, u32[]{:S(2)}) collective-permute-start(bf16[128,256]{1,0:T(8,128)(2,1)S(1)} %row_sum.2.refs_0_), channel_id=1, source_target_pairs={{0,6},{1,7},{2,4},{3,5},{4,2},{5,3},{6,0},{7,1},{8,14},{9,15},{10,... | collective-permute-start | bytes 196616 | tf_op jit(solution)/shard_map/ppermute | solution.py:496
  54.5 13.9 %sketch_pass.7 = (f32[1024,128]{1,0:T(8,128)S(1)}, bf16[32,1024,128]{2,1,0:T(8,128)(2,1)S(1)}) custom-call(s32[40]{0:T(128)S(1)} %get-tuple-element.45.order_ref, bf16[32,4096]{1,0:T(8,128)(2,1)S(1)} %get-tuple-element.32.src_pick, bf16[4096,128]{1,0:T(8,128)(2,1)S(1)} %get-tuple-element.33.omega_pick, bf16[4096,32]{1,0:T(8,128)(2,1)S(1)} %get-tuple-element.34.row_mat), custom_call_target="tpu_custom_call" | custom-call | flops 8589934592 | bytes 8388608 | tf_op jit(solution)/shard_map/sketch_pass/pallas_call | solution.py:232
  68.4 0.0 collective-permute-done.4.refs_1_
  68.4 0.0 collective-permute-done.5.refs_2_
  68.4 0.0 collective-permute-done.6.refs_3_
  68.5 0.1 collective-permute-start.7
  68.5 0.0 collective-permute-done.8.got_ref
  68.6 0.1 pair_sum.3
  68.6 0.1 collective-permute-start.10
  68.7 0.1 collective-permute-start.11
  68.8 3.4 %collective-permute-start.9 = (bf16[256,128]{1,0:T(8,128)(2,1)S(1)}, bf16[256,128]{1,0:T(8,128)(2,1)S(1)}, u32[]{:S(2)}, u32[]{:S(2)}) collective-permute-start(bf16[256,128]{1,0:T(8,128)(2,1)S(1)} %get-tuple-element.54), channel_id=1, source_target_pairs={{0,2},{1,3},{2,0},{3,1},{4,6},{5,7},{6,4},{7,5},{8,10},{9,11},{10,... | collective-permute-start | bytes 196616 | tf_op jit(solution)/shard_map/ppermute | solution.py:496
  72.2 3.7 %collective-permute-done.10.refs_1_ = bf16[256,128]{1,0:T(8,128)(2,1)S(1)} collective-permute-done((bf16[256,128]{1,0:T(8,128)(2,1)S(1)}, bf16[256,128]{1,0:T(8,128)(2,1)S(1)}, u32[]{:S(2)}, u32[]{:S(2)}) %collective-permute-start.10) | collective-permute-done | bytes 65568 | tf_op jit(solution)/shard_map/ppermute | solution.py:496
  75.9 0.0 collective-permute-done.11.refs_2_
  75.9 1.0 collective-permute-done.9.refs_0_
  76.9 0.1 row_sum.3.refs_0_.refs_1_.refs_2_
  77.0 0.6 collective-permute-start.12
  77.6 1.1 %collective-permute-start.13 = (bf16[128,256]{1,0:T(8,128)(2,1)S(1)}, bf16[128,256]{1,0:T(8,128)(2,1)S(1)}, u32[]{:S(2)}, u32[]{:S(2)}) collective-permute-start(bf16[128,256]{1,0:T(8,128)(2,1)S(1)} %row_sum.3.refs_0_.refs_1_.refs_2_), channel_id=1, source_target_pairs={{0,4},{1,5},{2,6},{3,7},{4,0},{5,1},{6,2},{7,3},{8,12},{9,13},{10,... | collective-permute-start | bytes 196616 | tf_op jit(solution)/shard_map/ppermute | solution.py:496
  78.8 2.7 %collective-permute-start.14 = (bf16[128,256]{1,0:T(8,128)(2,1)S(1)}, bf16[128,256]{1,0:T(8,128)(2,1)S(1)}, u32[]{:S(2)}, u32[]{:S(2)}) collective-permute-start(bf16[128,256]{1,0:T(8,128)(2,1)S(1)} %row_sum.3.refs_0_.refs_1_.refs_2_), channel_id=1, source_target_pairs={{0,6},{1,7},{2,4},{3,5},{4,2},{5,3},{6,0},{7,1},{8,14},{9,15},{10,... | collective-permute-start | bytes 196616 | tf_op jit(solution)/shard_map/ppermute | solution.py:496
  81.4 0.6 collective-permute-done.12.refs_1_.refs_3_
  82.0 3.6 %collective-permute-done.13.refs_2_.refs_4_ = bf16[128,256]{1,0:T(8,128)(2,1)S(1)} collective-permute-done((bf16[128,256]{1,0:T(8,128)(2,1)S(1)}, bf16[128,256]{1,0:T(8,128)(2,1)S(1)}, u32[]{:S(2)}, u32[]{:S(2)}) %collective-permute-start.13) | collective-permute-done | bytes 65568 | tf_op jit(solution)/shard_map/ppermute | solution.py:496
  85.6 0.0 collective-permute-done.14.refs_3_.refs_5_
  85.6 0.1 collective-permute-start.15
  85.7 0.0 collective-permute-done.7.odd_ref
  85.7 4.7 %first_pass.1 = (f32[128,4096]{1,0:T(8,128)S(1)}, f32[128,128]{1,0:T(8,128)S(1)}) custom-call(s32[40]{0:T(128)S(1)} %get-tuple-element.45.order_ref, bf16[4,128,256]{2,1,0:T(8,128)(2,1)S(1)} %collective-permute-done.7.odd_ref, bf16[128,256]{1,0:T(8,128)(2,1)S(1)} %row_sum.2.refs_0_, bf16[128,256]{1,0:T(8,128)(2,1)S(1)} %collective-permute-done.4.refs_1_, ...), custom_call_target="tpu_custom_call" | custom-call | flops 2147483648 | tf_op jit(solution)/shard_map/first_pass/pallas_call | solution.py:384
  90.4 0.0 collective-permute-done.15.odd_ref
  90.4 10.1 %project_pass.1 = (f32[512,128]{1,0:T(8,128)}, bf16[1,128,4096]{2,1,0:T(8,128)(2,1)}) custom-call(s32[40]{0:T(128)S(1)} %get-tuple-element.45.order_ref, f32[128,4096]{1,0:T(8,128)S(1)} %get-tuple-element.50.first_ref, f32[128,128]{1,0:T(8,128)S(1)} %get-tuple-element.51.gram_ref, bf16[4,128,256]{2,1,0:T(8,128)(2,1)S(1)} %collective-permute-done.15.odd_ref, ...), custom_call_target="tpu_custom_call" | custom-call | tf_op jit(solution)/shard_map/project_pass/pallas_call | solution.py:458
  (2 shorter events, 0.0 us)
Async XLA Ops:
  17.4 14.0 %collective-permute-start = (f32[1024,128]{1,0:T(8,128)S(1)}, f32[1024,128]{1,0:T(8,128)S(1)}, u32[]{:S(2)}, u32[]{:S(2)}) collective-permute-start(f32[1024,128]{1,0:T(8,128)S(1)} %get-tuple-element.35), channel_id=1, source_target_pairs={{0,1},{1,0},{2,3},{3,2},{4,5},{5,4},{6,7},{7,6},{8,9},{9,8},{10,11... | collective-permute-start | bytes 1572872 | tf_op jit(solution)/shard_map/ppermute | solution.py:496
  31.5 18.4 %collective-permute-start.1 = (bf16[256,128]{1,0:T(8,128)(2,1)S(1)}, bf16[256,128]{1,0:T(8,128)(2,1)S(1)}, u32[]{:S(2)}, u32[]{:S(2)}) collective-permute-start(bf16[256,128]{1,0:T(8,128)(2,1)S(1)} %get-tuple-element.42), channel_id=1, source_target_pairs={{0,2},{1,3},{2,0},{3,1},{4,6},{5,7},{6,4},{7,5},{8,10},{9,11},{10,... | collective-permute-start | bytes 196616 | tf_op jit(solution)/shard_map/ppermute | solution.py:496
  31.6 18.4 %collective-permute-start.2 = (bf16[256,128]{1,0:T(8,128)(2,1)S(1)}, bf16[256,128]{1,0:T(8,128)(2,1)S(1)}, u32[]{:S(2)}, u32[]{:S(2)}) collective-permute-start(bf16[256,128]{1,0:T(8,128)(2,1)S(1)} %get-tuple-element.43), channel_id=1, source_target_pairs={{0,4},{1,5},{2,6},{3,7},{4,0},{5,1},{6,2},{7,3},{8,12},{9,13},{10,... | collective-permute-start | bytes 196616 | tf_op jit(solution)/shard_map/ppermute | solution.py:496
  31.7 18.3 %collective-permute-start.3 = (bf16[256,128]{1,0:T(8,128)(2,1)S(1)}, bf16[256,128]{1,0:T(8,128)(2,1)S(1)}, u32[]{:S(2)}, u32[]{:S(2)}) collective-permute-start(bf16[256,128]{1,0:T(8,128)(2,1)S(1)} %get-tuple-element.44), channel_id=1, source_target_pairs={{0,6},{1,7},{2,4},{3,5},{4,2},{5,3},{6,0},{7,1},{8,14},{9,15},{10,... | collective-permute-start | bytes 196616 | tf_op jit(solution)/shard_map/ppermute | solution.py:496
  49.8 18.7 %collective-permute-start.8 = (f32[1024,128]{1,0:T(8,128)S(1)}, f32[1024,128]{1,0:T(8,128)S(1)}, u32[]{:S(2)}, u32[]{:S(2)}) collective-permute-start(f32[1024,128]{1,0:T(8,128)S(1)} %get-tuple-element.40), channel_id=1, source_target_pairs={{0,1},{1,0},{2,3},{3,2},{4,5},{5,4},{6,7},{7,6},{8,9},{9,8},{10,11... | collective-permute-start | bytes 1572872 | tf_op jit(solution)/shard_map/ppermute | solution.py:496
  50.1 18.3 %collective-permute-start.4 = (bf16[128,256]{1,0:T(8,128)(2,1)S(1)}, bf16[128,256]{1,0:T(8,128)(2,1)S(1)}, u32[]{:S(2)}, u32[]{:S(2)}) collective-permute-start(bf16[128,256]{1,0:T(8,128)(2,1)S(1)} %row_sum.2.refs_0_), channel_id=1, source_target_pairs={{0,2},{1,3},{2,0},{3,1},{4,6},{5,7},{6,4},{7,5},{8,10},{9,11},{10,... | collective-permute-start | bytes 196616 | tf_op jit(solution)/shard_map/ppermute | solution.py:496
  50.1 18.3 %collective-permute-start.5 = (bf16[128,256]{1,0:T(8,128)(2,1)S(1)}, bf16[128,256]{1,0:T(8,128)(2,1)S(1)}, u32[]{:S(2)}, u32[]{:S(2)}) collective-permute-start(bf16[128,256]{1,0:T(8,128)(2,1)S(1)} %row_sum.2.refs_0_), channel_id=1, source_target_pairs={{0,4},{1,5},{2,6},{3,7},{4,0},{5,1},{6,2},{7,3},{8,12},{9,13},{10,... | collective-permute-start | bytes 196616 | tf_op jit(solution)/shard_map/ppermute | solution.py:496
  50.2 18.2 %collective-permute-start.6 = (bf16[128,256]{1,0:T(8,128)(2,1)S(1)}, bf16[128,256]{1,0:T(8,128)(2,1)S(1)}, u32[]{:S(2)}, u32[]{:S(2)}) collective-permute-start(bf16[128,256]{1,0:T(8,128)(2,1)S(1)} %row_sum.2.refs_0_), channel_id=1, source_target_pairs={{0,6},{1,7},{2,4},{3,5},{4,2},{5,3},{6,0},{7,1},{8,14},{9,15},{10,... | collective-permute-start | bytes 196616 | tf_op jit(solution)/shard_map/ppermute | solution.py:496
  68.5 17.2 %collective-permute-start.7 = (bf16[4,128,256]{2,1,0:T(8,128)(2,1)S(1)}, bf16[4,128,256]{2,1,0:T(8,128)(2,1)S(1)}, u32[]{:S(2)}, u32[]{:S(2)}) collective-permute-start(bf16[4,128,256]{2,1,0:T(8,128)(2,1)S(1)} %join.2), channel_id=1, source_target_pairs={{0,1},{1,0},{2,3},{3,2},{4,5},{5,4},{6,7},{7,6},{8,9},{9,8},{10,11... | collective-permute-start | bytes 786440 | tf_op jit(solution)/shard_map/ppermute | solution.py:496
  68.6 7.3 %collective-permute-start.10 = (bf16[256,128]{1,0:T(8,128)(2,1)S(1)}, bf16[256,128]{1,0:T(8,128)(2,1)S(1)}, u32[]{:S(2)}, u32[]{:S(2)}) collective-permute-start(bf16[256,128]{1,0:T(8,128)(2,1)S(1)} %get-tuple-element.55), channel_id=1, source_target_pairs={{0,4},{1,5},{2,6},{3,7},{4,0},{5,1},{6,2},{7,3},{8,12},{9,13},{10,... | collective-permute-start | bytes 196616 | tf_op jit(solution)/shard_map/ppermute | solution.py:496
  68.7 7.2 %collective-permute-start.11 = (bf16[256,128]{1,0:T(8,128)(2,1)S(1)}, bf16[256,128]{1,0:T(8,128)(2,1)S(1)}, u32[]{:S(2)}, u32[]{:S(2)}) collective-permute-start(bf16[256,128]{1,0:T(8,128)(2,1)S(1)} %get-tuple-element.56), channel_id=1, source_target_pairs={{0,6},{1,7},{2,4},{3,5},{4,2},{5,3},{6,0},{7,1},{8,14},{9,15},{10,... | collective-permute-start | bytes 196616 | tf_op jit(solution)/shard_map/ppermute | solution.py:496
  68.8 8.1 %collective-permute-start.9 = (bf16[256,128]{1,0:T(8,128)(2,1)S(1)}, bf16[256,128]{1,0:T(8,128)(2,1)S(1)}, u32[]{:S(2)}, u32[]{:S(2)}) collective-permute-start(bf16[256,128]{1,0:T(8,128)(2,1)S(1)} %get-tuple-element.54), channel_id=1, source_target_pairs={{0,2},{1,3},{2,0},{3,1},{4,6},{5,7},{6,4},{7,5},{8,10},{9,11},{10,... | collective-permute-start | bytes 196616 | tf_op jit(solution)/shard_map/ppermute | solution.py:496
  77.0 5.0 %collective-permute-start.12 = (bf16[128,256]{1,0:T(8,128)(2,1)S(1)}, bf16[128,256]{1,0:T(8,128)(2,1)S(1)}, u32[]{:S(2)}, u32[]{:S(2)}) collective-permute-start(bf16[128,256]{1,0:T(8,128)(2,1)S(1)} %row_sum.3.refs_0_.refs_1_.refs_2_), channel_id=1, source_target_pairs={{0,2},{1,3},{2,0},{3,1},{4,6},{5,7},{6,4},{7,5},{8,10},{9,11},{10,... | collective-permute-start | bytes 196616 | tf_op jit(solution)/shard_map/ppermute | solution.py:496
  77.6 8.0 %collective-permute-start.13 = (bf16[128,256]{1,0:T(8,128)(2,1)S(1)}, bf16[128,256]{1,0:T(8,128)(2,1)S(1)}, u32[]{:S(2)}, u32[]{:S(2)}) collective-permute-start(bf16[128,256]{1,0:T(8,128)(2,1)S(1)} %row_sum.3.refs_0_.refs_1_.refs_2_), channel_id=1, source_target_pairs={{0,4},{1,5},{2,6},{3,7},{4,0},{5,1},{6,2},{7,3},{8,12},{9,13},{10,... | collective-permute-start | bytes 196616 | tf_op jit(solution)/shard_map/ppermute | solution.py:496
  78.8 6.8 %collective-permute-start.14 = (bf16[128,256]{1,0:T(8,128)(2,1)S(1)}, bf16[128,256]{1,0:T(8,128)(2,1)S(1)}, u32[]{:S(2)}, u32[]{:S(2)}) collective-permute-start(bf16[128,256]{1,0:T(8,128)(2,1)S(1)} %row_sum.3.refs_0_.refs_1_.refs_2_), channel_id=1, source_target_pairs={{0,6},{1,7},{2,4},{3,5},{4,2},{5,3},{6,0},{7,1},{8,14},{9,15},{10,... | collective-permute-start | bytes 196616 | tf_op jit(solution)/shard_map/ppermute | solution.py:496
  85.6 4.8 %collective-permute-start.15 = (bf16[4,128,256]{2,1,0:T(8,128)(2,1)S(1)}, bf16[4,128,256]{2,1,0:T(8,128)(2,1)S(1)}, u32[]{:S(2)}, u32[]{:S(2)}) collective-permute-start(bf16[4,128,256]{2,1,0:T(8,128)(2,1)S(1)} %join.3), channel_id=1, source_target_pairs={{0,1},{1,0},{2,3},{3,2},{4,5},{5,4},{6,7},{7,6},{8,9},{9,8},{10,11... | collective-permute-start | bytes 786440 | tf_op jit(solution)/shard_map/ppermute | solution.py:496
where the time goes:
time: 101 us; the launch traced here: 100 us
  Pallas kernels  73.6 us (73%)
  starting transfers between devices  17.2 us (17%)
  waiting for transfers between devices  8.87 us (9%)
    pallas_call x4, Pallas kernels, sketch_pass(): pl.pallas_call(functools.partial(sketch_kernel, first=first, panels=panel...  55.5 us
    ppermute x16, starting transfers between devices, swap(): return lax.ppermute(x, 'tile', [(i, i ^ k) for i in range(n)])  17.2 us
    pallas_call x1, Pallas kernels, project_pass(): pl.pallas_call(functools.partial(project_kernel, panels=panels, half=len(...  10.1 us
    ppermute x16, waiting for transfers between devices, swap(): return lax.ppermute(x, 'tile', [(i, i ^ k) for i in range(n)])  8.87 us
    pallas_call x1, Pallas kernels, first_pass(): pl.pallas_call(functools.partial(first_kernel, panels=panels, half=len(ev...  4.65 us
    pallas_call x1, Pallas kernels, prep(): pl.pallas_call(functools.partial(prep_kernel, slices=slices, place=place)...  2.94 us
  transfers between devices with their start and end apart: 16, of which 4 were waited for; matrix products, arithmetic and copies ran while one was open for 0% of the time, Pallas kernels for 46%

commit v1 on v0

--- a/solution.py
+++ b/solution.py
@@ -25,7 +25,6 @@
 GROUP = 8
 FEW = 4
 HALF = FEW * WIDTH
-WHOLE = 1.5 * 2.0**23
 
 
 def head(x):
@@ -62,7 +61,7 @@
 def near_field(square):
     inv = lax.rsqrt(square)
     t = square * inv
-    f = t - ((t + WHOLE) - WHOLE)
+    f = t - jnp.round(t)
     g = 0.25 - jnp.abs(f)
     v = g * g
     wave = ((S2 * v + S1) * v + S0) * g
@@ -227,7 +226,7 @@
 
 def sketch_pass(order, src_pick, omega_pick, row_mat, first, rows, panels):
     rank = omega_pick.shape[1]
-    rb = min(512, rows)
+    rb = min(1024, rows)
     vmem = pl.BlockSpec(memory_space=pltpu.VMEM)
     return pl.pallas_call(
         functools.partial(sketch_kernel, first=first, panels=panels, rb=rb),
@@ -545,13 +544,17 @@
         tiles.append(kept)
         sums = sum_cores(got, after(own, *(x for h in held[-1:] for x in h)))
         last = (own, sums[0])
-    held.append(along_z(*sums))
     rank = sketch.shape[1]
-    odds = [swap(join([after(h[0], own), *h[1:]]), 1, n) for h in held]
-    first, gram = first_pass(order, odds[0], held[0], tiles[:2], panels, rank, flip)
+
+    def across(pieces, *deps):
+        return swap(join([after(pieces[0], *deps), *pieces[1:]]), 1, n)
+
+    odd = across(held[0], own)
+    first, gram = first_pass(order, odd, held[0], tiles[:2], panels, rank, flip)
+    held.append(along_z(after(sums[0], gram), sums[1]))
     owns = [h[0] for h in held]
     return project_pass(
-        order, first, gram, odds[1], owns, held[1], tiles[2:], panels, rank, flip
+        order, first, gram, across(held[1]), owns, held[1], tiles[2:], panels, rank, flip
     )
 
 

time: 101 us -> 88.7 us (0.88)
  Pallas kernels: 73.6 us -> 13.1 us
  starting transfers between devices: 17.2 us -> 51.5 us
  waiting for transfers between devices: 8.87 us -> 22.2 us
    pallas_call x4, Pallas kernels: 55.5 us -> 2.62 us  [sketch_pass(): pl.pallas_call(functools.partial(sketch_kernel, first=first, panels=panel...]
    ppermute x16, starting transfers between devices: 17.2 us -> 51.5 us  [swap(): return lax.ppermute(x, 'tile', [(i, i ^ k) for i in range(n)])]
    ppermute x16, waiting for transfers between devices: 8.87 us -> 22.2 us  [swap(): return lax.ppermute(x, 'tile', [(i, i ^ k) for i in range(n)])]
    pallas_call x1, Pallas kernels: 4.65 us -> 0.83 us  [first_pass(): pl.pallas_call(functools.partial(first_kernel, panels=panels, half=len(ev...]
    pallas_call x1, Pallas kernels: 10.1 us -> 6.97 us  [project_pass(): pl.pallas_call(functools.partial(project_kernel, panels=panels, half=len(...]
  transfers between devices with their start and end apart: 16 -> 16, of which waited for: 4 -> 10; matrix products, arithmetic and copies ran while one was open for 0% -> 0% of each run, Pallas kernels for 46% -> 3%
where the time goes in v1:
time: 88.7 us; the launch traced here: 87.5 us
  starting transfers between devices  51.5 us (58%)
  waiting for transfers between devices  22.2 us (25%)
  Pallas kernels  13.1 us (15%)
    ppermute x16, starting transfers between devices, swap(): return lax.ppermute(x, 'tile', [(i, i ^ k) for i in range(n)])  51.5 us
    ppermute x16, waiting for transfers between devices, swap(): return lax.ppermute(x, 'tile', [(i, i ^ k) for i in range(n)])  22.2 us
    pallas_call x1, Pallas kernels, project_pass(): pl.pallas_call(functools.partial(project_kernel, panels=panels, half=len(...  6.97 us
    pallas_call x4, Pallas kernels, sketch_pass(): pl.pallas_call(functools.partial(sketch_kernel, first=first, panels=panel...  2.62 us
    pallas_call x1, Pallas kernels, prep(): pl.pallas_call(functools.partial(prep_kernel, slices=slices, place=place)...  2.29 us
  transfers between devices with their start and end apart: 16, of which 10 were waited for; matrix products, arithmetic and copies ran while one was open for 0% of the time, Pallas kernels for 3%

profile of v1, /device:TPU:0, one launch (start us, length us, event | category | flops | bytes accessed | tf_op | source)
XLA Modules:
  0.0 87.5 jit_solution(9979298273059905970)
XLA Ops:
  0.6 2.3 %prep.1 = (s32[40]{0:T(128)S(1)}, bf16[32,4096]{1,0:T(8,128)(2,1)S(1)}, bf16[4096,128]{1,0:T(8,128)(2,1)S(1)}, bf16[4096,32]{1,0:T(8,128)(2,1)S(1)}) custom-call(s32[1,32]{1,0:T(1,128)} %flags_hbm.1, f32[3,16384]{1,0:T(4,128)} %rows_hbm.1, f32[3,4096]{1,0:T(4,128)} %src_hbm.1, bf16[4096,128]{1,0:T(8,128)(2,1)} %omega_hbm.1), custom_call_target="tpu_custom_call" | custom-call | tf_op jit(solution)/shard_map/prep/pallas_call | solution.py:165
  2.9 0.6 sketch_pass.4
  3.5 0.5 collective-permute-start
  4.1 0.6 sketch_pass.5
  4.7 0.9 %collective-permute-done.got_ref = f32[1024,128]{1,0:T(8,128)S(1)} collective-permute-done((f32[1024,128]{1,0:T(8,128)S(1)}, f32[1024,128]{1,0:T(8,128)S(1)}, u32[]{:S(2)}, u32[]{:S(2)}) %collective-permute-start) | collective-permute-done | bytes 524320 | tf_op jit(solution)/shard_map/ppermute | solution.py:495
  5.6 0.1 pair_sum.2
  5.7 21.1 %collective-permute-start.1 = (bf16[256,128]{1,0:T(8,128)(2,1)S(1)}, bf16[256,128]{1,0:T(8,128)(2,1)S(1)}, u32[]{:S(2)}, u32[]{:S(2)}) collective-permute-start(bf16[256,128]{1,0:T(8,128)(2,1)S(1)} %get-tuple-element.42), channel_id=1, source_target_pairs={{0,2},{1,3},{2,0},{3,1},{4,6},{5,7},{6,4},{7,5},{8,10},{9,11},{10,... | collective-permute-start | bytes 196616 | tf_op jit(solution)/shard_map/ppermute | solution.py:495
  26.7 5.4 %collective-permute-start.2 = (bf16[256,128]{1,0:T(8,128)(2,1)S(1)}, bf16[256,128]{1,0:T(8,128)(2,1)S(1)}, u32[]{:S(2)}, u32[]{:S(2)}) collective-permute-start(bf16[256,128]{1,0:T(8,128)(2,1)S(1)} %get-tuple-element.43), channel_id=1, source_target_pairs={{0,4},{1,5},{2,6},{3,7},{4,0},{5,1},{6,2},{7,3},{8,12},{9,13},{10,... | collective-permute-start | bytes 196616 | tf_op jit(solution)/shard_map/ppermute | solution.py:495
  32.1 0.0 collective-permute-start.3
  32.1 0.6 sketch_pass.6
  32.7 0.1 collective-permute-start.8
  32.8 0.0 collective-permute-done.1.refs_0_
  32.8 3.6 %collective-permute-done.2.refs_1_ = bf16[256,128]{1,0:T(8,128)(2,1)S(1)} collective-permute-done((bf16[256,128]{1,0:T(8,128)(2,1)S(1)}, bf16[256,128]{1,0:T(8,128)(2,1)S(1)}, u32[]{:S(2)}, u32[]{:S(2)}) %collective-permute-start.2) | collective-permute-done | bytes 65568 | tf_op jit(solution)/shard_map/ppermute | solution.py:495
  36.4 1.7 %collective-permute-done.3.refs_2_ = bf16[256,128]{1,0:T(8,128)(2,1)S(1)} collective-permute-done((bf16[256,128]{1,0:T(8,128)(2,1)S(1)}, bf16[256,128]{1,0:T(8,128)(2,1)S(1)}, u32[]{:S(2)}, u32[]{:S(2)}) %collective-permute-start.3) | collective-permute-done | bytes 65568 | tf_op jit(solution)/shard_map/ppermute | solution.py:495
  38.2 0.1 row_sum.2.refs_0_
  38.3 5.5 %collective-permute-start.4 = (bf16[128,256]{1,0:T(8,128)(2,1)S(1)}, bf16[128,256]{1,0:T(8,128)(2,1)S(1)}, u32[]{:S(2)}, u32[]{:S(2)}) collective-permute-start(bf16[128,256]{1,0:T(8,128)(2,1)S(1)} %row_sum.2.refs_0_), channel_id=1, source_target_pairs={{0,2},{1,3},{2,0},{3,1},{4,6},{5,7},{6,4},{7,5},{8,10},{9,11},{10,... | collective-permute-start | bytes 196616 | tf_op jit(solution)/shard_map/ppermute | solution.py:495
  43.7 4.4 %collective-permute-start.5 = (bf16[128,256]{1,0:T(8,128)(2,1)S(1)}, bf16[128,256]{1,0:T(8,128)(2,1)S(1)}, u32[]{:S(2)}, u32[]{:S(2)}) collective-permute-start(bf16[128,256]{1,0:T(8,128)(2,1)S(1)} %row_sum.2.refs_0_), channel_id=1, source_target_pairs={{0,4},{1,5},{2,6},{3,7},{4,0},{5,1},{6,2},{7,3},{8,12},{9,13},{10,... | collective-permute-start | bytes 196616 | tf_op jit(solution)/shard_map/ppermute | solution.py:495
  48.2 0.0 collective-permute-start.6
  48.2 0.8 sketch_pass.7
  49.0 0.0 collective-permute-done.4.refs_1_
  49.0 3.4 %collective-permute-done.5.refs_2_ = bf16[128,256]{1,0:T(8,128)(2,1)S(1)} collective-permute-done((bf16[128,256]{1,0:T(8,128)(2,1)S(1)}, bf16[128,256]{1,0:T(8,128)(2,1)S(1)}, u32[]{:S(2)}, u32[]{:S(2)}) %collective-permute-start.5) | collective-permute-done | bytes 65568 | tf_op jit(solution)/shard_map/ppermute | solution.py:495
  52.4 1.9 %collective-permute-done.6.refs_3_ = bf16[128,256]{1,0:T(8,128)(2,1)S(1)} collective-permute-done((bf16[128,256]{1,0:T(8,128)(2,1)S(1)}, bf16[128,256]{1,0:T(8,128)(2,1)S(1)}, u32[]{:S(2)}, u32[]{:S(2)}) %collective-permute-start.6) | collective-permute-done | bytes 65568 | tf_op jit(solution)/shard_map/ppermute | solution.py:495
  54.3 0.1 collective-permute-start.7
  54.4 0.0 collective-permute-done.8.got_ref
  54.4 0.1 pair_sum.3
  54.5 4.4 %collective-permute-start.10 = (bf16[256,128]{1,0:T(8,128)(2,1)S(1)}, bf16[256,128]{1,0:T(8,128)(2,1)S(1)}, u32[]{:S(2)}, u32[]{:S(2)}) collective-permute-start(bf16[256,128]{1,0:T(8,128)(2,1)S(1)} %get-tuple-element.56), channel_id=1, source_target_pairs={{0,4},{1,5},{2,6},{3,7},{4,0},{5,1},{6,2},{7,3},{8,12},{9,13},{10,... | collective-permute-start | bytes 196616 | tf_op jit(solution)/shard_map/ppermute | solution.py:495
  58.9 5.1 %collective-permute-start.11 = (bf16[256,128]{1,0:T(8,128)(2,1)S(1)}, bf16[256,128]{1,0:T(8,128)(2,1)S(1)}, u32[]{:S(2)}, u32[]{:S(2)}) collective-permute-start(bf16[256,128]{1,0:T(8,128)(2,1)S(1)} %get-tuple-element.57), channel_id=1, source_target_pairs={{0,6},{1,7},{2,4},{3,5},{4,2},{5,3},{6,0},{7,1},{8,14},{9,15},{10,... | collective-permute-start | bytes 196616 | tf_op jit(solution)/shard_map/ppermute | solution.py:495
  63.9 0.5 collective-permute-start.9
  64.4 0.0 collective-permute-done.7.odd_ref
  64.4 0.8 first_pass.1
  65.3 0.0 collective-permute-done.10.refs_1_
  65.3 2.9 %collective-permute-done.11.refs_2_ = bf16[256,128]{1,0:T(8,128)(2,1)S(1)} collective-permute-done((bf16[256,128]{1,0:T(8,128)(2,1)S(1)}, bf16[256,128]{1,0:T(8,128)(2,1)S(1)}, u32[]{:S(2)}, u32[]{:S(2)}) %collective-permute-start.11) | collective-permute-done | bytes 65568 | tf_op jit(solution)/shard_map/ppermute | solution.py:495
  68.2 1.2 %collective-permute-done.9.refs_0_ = bf16[256,128]{1,0:T(8,128)(2,1)S(1)} collective-permute-done((bf16[256,128]{1,0:T(8,128)(2,1)S(1)}, bf16[256,128]{1,0:T(8,128)(2,1)S(1)}, u32[]{:S(2)}, u32[]{:S(2)}) %collective-permute-start.9) | collective-permute-done | bytes 65568 | tf_op jit(solution)/shard_map/ppermute | solution.py:495
  69.4 0.1 row_sum.3.refs_0_.refs_1_.refs_2_
  69.5 0.7 collective-permute-start.12
  70.1 2.6 %collective-permute-start.13 = (bf16[128,256]{1,0:T(8,128)(2,1)S(1)}, bf16[128,256]{1,0:T(8,128)(2,1)S(1)}, u32[]{:S(2)}, u32[]{:S(2)}) collective-permute-start(bf16[128,256]{1,0:T(8,128)(2,1)S(1)} %row_sum.3.refs_0_.refs_1_.refs_2_), channel_id=1, source_target_pairs={{0,4},{1,5},{2,6},{3,7},{4,0},{5,1},{6,2},{7,3},{8,12},{9,13},{10,... | collective-permute-start | bytes 196616 | tf_op jit(solution)/shard_map/ppermute | solution.py:495
  72.8 1.2 %collective-permute-start.14 = (bf16[128,256]{1,0:T(8,128)(2,1)S(1)}, bf16[128,256]{1,0:T(8,128)(2,1)S(1)}, u32[]{:S(2)}, u32[]{:S(2)}) collective-permute-start(bf16[128,256]{1,0:T(8,128)(2,1)S(1)} %row_sum.3.refs_0_.refs_1_.refs_2_), channel_id=1, source_target_pairs={{0,6},{1,7},{2,4},{3,5},{4,2},{5,3},{6,0},{7,1},{8,14},{9,15},{10,... | collective-permute-start | bytes 196616 | tf_op jit(solution)/shard_map/ppermute | solution.py:495
  73.9 0.0 collective-permute-done.12.refs_1_.refs_3_
  73.9 3.9 %collective-permute-done.13.refs_2_.refs_4_ = bf16[128,256]{1,0:T(8,128)(2,1)S(1)} collective-permute-done((bf16[128,256]{1,0:T(8,128)(2,1)S(1)}, bf16[128,256]{1,0:T(8,128)(2,1)S(1)}, u32[]{:S(2)}, u32[]{:S(2)}) %collective-permute-start.13) | collective-permute-done | bytes 65568 | tf_op jit(solution)/shard_map/ppermute | solution.py:495
  77.8 1.2 %collective-permute-done.14.refs_3_.refs_5_ = bf16[128,256]{1,0:T(8,128)(2,1)S(1)} collective-permute-done((bf16[128,256]{1,0:T(8,128)(2,1)S(1)}, bf16[128,256]{1,0:T(8,128)(2,1)S(1)}, u32[]{:S(2)}, u32[]{:S(2)}) %collective-permute-start.14) | collective-permute-done | bytes 65568 | tf_op jit(solution)/shard_map/ppermute | solution.py:495
  79.0 0.1 collective-permute-start.15
  79.0 1.5 %collective-permute-done.15.odd_ref = bf16[4,128,256]{2,1,0:T(8,128)(2,1)S(1)} collective-permute-done((bf16[4,128,256]{2,1,0:T(8,128)(2,1)S(1)}, bf16[4,128,256]{2,1,0:T(8,128)(2,1)S(1)}, u32[]{:S(2)}, u32[]{:S(2)}) %collective-permute-start.15) | collective-permute-done | bytes 262176 | tf_op jit(solution)/shard_map/ppermute | solution.py:495
  80.6 7.0 %project_pass.1 = (f32[512,128]{1,0:T(8,128)}, bf16[1,128,4096]{2,1,0:T(8,128)(2,1)}) custom-call(s32[40]{0:T(128)S(1)} %get-tuple-element.45.order_ref, f32[128,4096]{1,0:T(8,128)S(1)} %get-tuple-element.50.first_ref, f32[128,128]{1,0:T(8,128)S(1)} %get-tuple-element.51.gram_ref, bf16[4,128,256]{2,1,0:T(8,128)(2,1)S(1)} %collective-permute-done.15.odd_ref, ...), custom_call_target="tpu_custom_call" | custom-call | tf_op jit(solution)/shard_map/project_pass/pallas_call | solution.py:457
  (2 shorter events, 0.0 us)
Async XLA Ops:
  3.5 2.1 %collective-permute-start = (f32[1024,128]{1,0:T(8,128)S(1)}, f32[1024,128]{1,0:T(8,128)S(1)}, u32[]{:S(2)}, u32[]{:S(2)}) collective-permute-start(f32[1024,128]{1,0:T(8,128)S(1)} %get-tuple-element.35), channel_id=1, source_target_pairs={{0,1},{1,0},{2,3},{3,2},{4,5},{5,4},{6,7},{7,6},{8,9},{9,8},{10,11... | collective-permute-start | bytes 1572872 | tf_op jit(solution)/shard_map/ppermute | solution.py:495
  5.7 27.2 %collective-permute-start.1 = (bf16[256,128]{1,0:T(8,128)(2,1)S(1)}, bf16[256,128]{1,0:T(8,128)(2,1)S(1)}, u32[]{:S(2)}, u32[]{:S(2)}) collective-permute-start(bf16[256,128]{1,0:T(8,128)(2,1)S(1)} %get-tuple-element.42), channel_id=1, source_target_pairs={{0,2},{1,3},{2,0},{3,1},{4,6},{5,7},{6,4},{7,5},{8,10},{9,11},{10,... | collective-permute-start | bytes 196616 | tf_op jit(solution)/shard_map/ppermute | solution.py:495
  26.7 9.7 %collective-permute-start.2 = (bf16[256,128]{1,0:T(8,128)(2,1)S(1)}, bf16[256,128]{1,0:T(8,128)(2,1)S(1)}, u32[]{:S(2)}, u32[]{:S(2)}) collective-permute-start(bf16[256,128]{1,0:T(8,128)(2,1)S(1)} %get-tuple-element.43), channel_id=1, source_target_pairs={{0,4},{1,5},{2,6},{3,7},{4,0},{5,1},{6,2},{7,3},{8,12},{9,13},{10,... | collective-permute-start | bytes 196616 | tf_op jit(solution)/shard_map/ppermute | solution.py:495
  32.1 6.1 %collective-permute-start.3 = (bf16[256,128]{1,0:T(8,128)(2,1)S(1)}, bf16[256,128]{1,0:T(8,128)(2,1)S(1)}, u32[]{:S(2)}, u32[]{:S(2)}) collective-permute-start(bf16[256,128]{1,0:T(8,128)(2,1)S(1)} %get-tuple-element.44), channel_id=1, source_target_pairs={{0,6},{1,7},{2,4},{3,5},{4,2},{5,3},{6,0},{7,1},{8,14},{9,15},{10,... | collective-permute-start | bytes 196616 | tf_op jit(solution)/shard_map/ppermute | solution.py:495
  32.7 21.7 %collective-permute-start.8 = (f32[1024,128]{1,0:T(8,128)S(1)}, f32[1024,128]{1,0:T(8,128)S(1)}, u32[]{:S(2)}, u32[]{:S(2)}) collective-permute-start(f32[1024,128]{1,0:T(8,128)S(1)} %get-tuple-element.40), channel_id=1, source_target_pairs={{0,1},{1,0},{2,3},{3,2},{4,5},{5,4},{6,7},{7,6},{8,9},{9,8},{10,11... | collective-permute-start | bytes 1572872 | tf_op jit(solution)/shard_map/ppermute | solution.py:495
  38.3 10.7 %collective-permute-start.4 = (bf16[128,256]{1,0:T(8,128)(2,1)S(1)}, bf16[128,256]{1,0:T(8,128)(2,1)S(1)}, u32[]{:S(2)}, u32[]{:S(2)}) collective-permute-start(bf16[128,256]{1,0:T(8,128)(2,1)S(1)} %row_sum.2.refs_0_), channel_id=1, source_target_pairs={{0,2},{1,3},{2,0},{3,1},{4,6},{5,7},{6,4},{7,5},{8,10},{9,11},{10,... | collective-permute-start | bytes 196616 | tf_op jit(solution)/shard_map/ppermute | solution.py:495
  43.7 8.6 %collective-permute-start.5 = (bf16[128,256]{1,0:T(8,128)(2,1)S(1)}, bf16[128,256]{1,0:T(8,128)(2,1)S(1)}, u32[]{:S(2)}, u32[]{:S(2)}) collective-permute-start(bf16[128,256]{1,0:T(8,128)(2,1)S(1)} %row_sum.2.refs_0_), channel_id=1, source_target_pairs={{0,4},{1,5},{2,6},{3,7},{4,0},{5,1},{6,2},{7,3},{8,12},{9,13},{10,... | collective-permute-start | bytes 196616 | tf_op jit(solution)/shard_map/ppermute | solution.py:495
  48.2 6.1 %collective-permute-start.6 = (bf16[128,256]{1,0:T(8,128)(2,1)S(1)}, bf16[128,256]{1,0:T(8,128)(2,1)S(1)}, u32[]{:S(2)}, u32[]{:S(2)}) collective-permute-start(bf16[128,256]{1,0:T(8,128)(2,1)S(1)} %row_sum.2.refs_0_), channel_id=1, source_target_pairs={{0,6},{1,7},{2,4},{3,5},{4,2},{5,3},{6,0},{7,1},{8,14},{9,15},{10,... | collective-permute-start | bytes 196616 | tf_op jit(solution)/shard_map/ppermute | solution.py:495
  54.3 10.1 %collective-permute-start.7 = (bf16[4,128,256]{2,1,0:T(8,128)(2,1)S(1)}, bf16[4,128,256]{2,1,0:T(8,128)(2,1)S(1)}, u32[]{:S(2)}, u32[]{:S(2)}) collective-permute-start(bf16[4,128,256]{2,1,0:T(8,128)(2,1)S(1)} %join.2), channel_id=1, source_target_pairs={{0,1},{1,0},{2,3},{3,2},{4,5},{5,4},{6,7},{7,6},{8,9},{9,8},{10,11... | collective-permute-start | bytes 786440 | tf_op jit(solution)/shard_map/ppermute | solution.py:495
  54.5 10.8 %collective-permute-start.10 = (bf16[256,128]{1,0:T(8,128)(2,1)S(1)}, bf16[256,128]{1,0:T(8,128)(2,1)S(1)}, u32[]{:S(2)}, u32[]{:S(2)}) collective-permute-start(bf16[256,128]{1,0:T(8,128)(2,1)S(1)} %get-tuple-element.56), channel_id=1, source_target_pairs={{0,4},{1,5},{2,6},{3,7},{4,0},{5,1},{6,2},{7,3},{8,12},{9,13},{10,... | collective-permute-start | bytes 196616 | tf_op jit(solution)/shard_map/ppermute | solution.py:495
  58.9 9.3 %collective-permute-start.11 = (bf16[256,128]{1,0:T(8,128)(2,1)S(1)}, bf16[256,128]{1,0:T(8,128)(2,1)S(1)}, u32[]{:S(2)}, u32[]{:S(2)}) collective-permute-start(bf16[256,128]{1,0:T(8,128)(2,1)S(1)} %get-tuple-element.57), channel_id=1, source_target_pairs={{0,6},{1,7},{2,4},{3,5},{4,2},{5,3},{6,0},{7,1},{8,14},{9,15},{10,... | collective-permute-start | bytes 196616 | tf_op jit(solution)/shard_map/ppermute | solution.py:495
  63.9 5.4 %collective-permute-start.9 = (bf16[256,128]{1,0:T(8,128)(2,1)S(1)}, bf16[256,128]{1,0:T(8,128)(2,1)S(1)}, u32[]{:S(2)}, u32[]{:S(2)}) collective-permute-start(bf16[256,128]{1,0:T(8,128)(2,1)S(1)} %get-tuple-element.55), channel_id=1, source_target_pairs={{0,2},{1,3},{2,0},{3,1},{4,6},{5,7},{6,4},{7,5},{8,10},{9,11},{10,... | collective-permute-start | bytes 196616 | tf_op jit(solution)/shard_map/ppermute | solution.py:495
  69.5 4.5 %collective-permute-start.12 = (bf16[128,256]{1,0:T(8,128)(2,1)S(1)}, bf16[128,256]{1,0:T(8,128)(2,1)S(1)}, u32[]{:S(2)}, u32[]{:S(2)}) collective-permute-start(bf16[128,256]{1,0:T(8,128)(2,1)S(1)} %row_sum.3.refs_0_.refs_1_.refs_2_), channel_id=1, source_target_pairs={{0,2},{1,3},{2,0},{3,1},{4,6},{5,7},{6,4},{7,5},{8,10},{9,11},{10,... | collective-permute-start | bytes 196616 | tf_op jit(solution)/shard_map/ppermute | solution.py:495
  70.1 7.6 %collective-permute-start.13 = (bf16[128,256]{1,0:T(8,128)(2,1)S(1)}, bf16[128,256]{1,0:T(8,128)(2,1)S(1)}, u32[]{:S(2)}, u32[]{:S(2)}) collective-permute-start(bf16[128,256]{1,0:T(8,128)(2,1)S(1)} %row_sum.3.refs_0_.refs_1_.refs_2_), channel_id=1, source_target_pairs={{0,4},{1,5},{2,6},{3,7},{4,0},{5,1},{6,2},{7,3},{8,12},{9,13},{10,... | collective-permute-start | bytes 196616 | tf_op jit(solution)/shard_map/ppermute | solution.py:495
  72.8 6.2 %collective-permute-start.14 = (bf16[128,256]{1,0:T(8,128)(2,1)S(1)}, bf16[128,256]{1,0:T(8,128)(2,1)S(1)}, u32[]{:S(2)}, u32[]{:S(2)}) collective-permute-start(bf16[128,256]{1,0:T(8,128)(2,1)S(1)} %row_sum.3.refs_0_.refs_1_.refs_2_), channel_id=1, source_target_pairs={{0,6},{1,7},{2,4},{3,5},{4,2},{5,3},{6,0},{7,1},{8,14},{9,15},{10,... | collective-permute-start | bytes 196616 | tf_op jit(solution)/shard_map/ppermute | solution.py:495
  79.0 1.6 %collective-permute-start.15 = (bf16[4,128,256]{2,1,0:T(8,128)(2,1)S(1)}, bf16[4,128,256]{2,1,0:T(8,128)(2,1)S(1)}, u32[]{:S(2)}, u32[]{:S(2)}) collective-permute-start(bf16[4,128,256]{2,1,0:T(8,128)(2,1)S(1)} %join.3), channel_id=1, source_target_pairs={{0,1},{1,0},{2,3},{3,2},{4,5},{5,4},{6,7},{7,6},{8,9},{9,8},{10,11... | collective-permute-start | bytes 786440 | tf_op jit(solution)/shard_map/ppermute | solution.py:495

commit v2 on v1

--- a/solution.py
+++ b/solution.py
@@ -22,7 +22,7 @@
 TERMS = 32
 SUB = 8
 PIECE = 16
-GROUP = 8
+GROUP = 16
 FEW = 4
 HALF = FEW * WIDTH
 
@@ -226,7 +226,7 @@
 
 def sketch_pass(order, src_pick, omega_pick, row_mat, first, rows, panels):
     rank = omega_pick.shape[1]
-    rb = min(1024, rows)
+    rb = min(512, rows)
     vmem = pl.BlockSpec(memory_space=pltpu.VMEM)
     return pl.pallas_call(
         functools.partial(sketch_kernel, first=first, panels=panels, rb=rb),
@@ -262,22 +262,22 @@
     return call
 
 
-def pair_sum_kernel(own_ref, got_ref, kept_ref, *sent_refs):
-    q = kept_ref.shape[0]
-    for k in range(1 + len(sent_refs)):
-        part = slice(k * q, (k + 1) * q)
-        value = own_ref[part, :] + got_ref[part, :]
-        if k == 0:
-            kept_ref[...] = value
-        else:
-            sent_refs[k - 1][...] = value.astype(jnp.bfloat16)
-
-
-def pair_sum(own, got, slots):
-    q, rank = own.shape[0] // slots, own.shape[1]
+def pair_sum_kernel(*refs, parts):
+    own_refs, got_refs, out_refs = refs[:parts], refs[parts : 2 * parts], refs[2 * parts :]
+    q = out_refs[0].shape[0]
+    each = len(out_refs) // parts
+    for k, out_ref in enumerate(out_refs):
+        rows = slice(k % each * q, (k % each + 1) * q)
+        value = own_refs[k // each][rows, :] + got_refs[k // each][rows, :]
+        out_ref[...] = value.astype(out_ref.dtype)
+
+
+def pair_sum(owns, gots, slots):
+    q, rank = sum(x.shape[0] for x in owns) // slots, owns[0].shape[1]
     shapes = [jax.ShapeDtypeStruct((q, rank), jnp.float32)]
     shapes += [jax.ShapeDtypeStruct((q, rank), jnp.bfloat16)] * (slots - 1)
-    return in_vmem(pair_sum_kernel, shapes, "pair_sum")(own, got)
+    kernel = functools.partial(pair_sum_kernel, parts=len(owns))
+    return in_vmem(kernel, shapes, "pair_sum")(*owns, *gots)
 
 
 def row_sum_kernel(kept_ref, *refs):
@@ -518,40 +518,49 @@
         admissible, points, source_points, sketch, rows, slices, place
     )
 
-    call_rows = rows // CHUNKS // 2
-
-    def sketch_part(at, *deps):
-        return sketch_pass(
-            after(order, *deps), src_pick, omega_pick, row_mat, at * call_rows, call_rows, panels
-        )
-
-    def sum_cores(got, own):
-        kept, *sent = pair_sum(own, got, n // 2)
-        return kept, [swap(x, k, n) for x, k in zip(sent, even[1:])]
-
-    def along_z(kept, got):
-        low = row_sum(kept, got, flip)
-        return [low] + [swap(low, k, n) for k in even[1:]]
-
-    held, tiles, sums, last = [], [], None, ()
-    for c in range(CHUNKS):
-        theirs, kept = sketch_part(2 * c, *last)
-        tiles.append(kept)
-        got = swap(theirs, 1, n)
-        if c > 0:
-            held.append(along_z(after(sums[0], theirs), sums[1]))
-        own, kept = sketch_part(2 * c + 1, theirs, *[h[0] for h in held[-1:]])
-        tiles.append(kept)
-        sums = sum_cores(got, after(own, *(x for h in held[-1:] for x in h)))
-        last = (own, sums[0])
+    half_rows = rows // CHUNKS // 2
+
+    def sketch_part(first, size, *deps):
+        return sketch_pass(after(order, *deps), src_pick, omega_pick, row_mat, first, size, panels)
+
+    def z_swaps(parts, *deps):
+        got = []
+        for x, k in zip(parts, even[1:]):
+            if deps and k == even[-1]:
+                x = after(x, *deps, *got)
+            got.append(swap(x, k, n))
+        return got
+
+    def along_z(low, *deps):
+        return [low, *z_swaps([low] * (n // 2 - 1), *deps)]
+
+    theirs, kept0 = sketch_part(0, half_rows)
+    got = swap(theirs, 1, n)
+    own, kept1 = sketch_part(half_rows, half_rows, theirs)
+    kept, *sent = pair_sum([own], [got], n // 2)
+
+    part = half_rows // 2
+    start = 2 * half_rows
+    theirs_a, kept2 = sketch_part(start, part, own, kept)
+    got_z = z_swaps(sent, theirs_a)
+    got_a = swap(theirs_a, 1, n)
+    theirs_b, kept3 = sketch_part(start + part, part, theirs_a)
+    got_b = swap(theirs_b, 1, n)
+    low = row_sum(after(kept, theirs_b), got_z, flip)
+    own_a, kept4 = sketch_part(start + 2 * part, part, theirs_b, low)
+    held = [along_z(low, own_a)]
+    own_b, kept5 = sketch_part(start + 3 * part, part, own_a)
+    kept, *sent = pair_sum([own_a, after(own_b, *held[0])], [got_a, got_b], n // 2)
+    tiles = [kept0, kept1, kept2, kept3, kept4, kept5]
     rank = sketch.shape[1]
 
     def across(pieces, *deps):
         return swap(join([after(pieces[0], *deps), *pieces[1:]]), 1, n)
 
-    odd = across(held[0], own)
+    odd = across(held[0], own_b)
     first, gram = first_pass(order, odd, held[0], tiles[:2], panels, rank, flip)
-    held.append(along_z(after(sums[0], gram), sums[1]))
+    got_z = z_swaps(sent, gram)
+    held.append(along_z(row_sum(kept, got_z, flip)))
     owns = [h[0] for h in held]
     return project_pass(
         order, first, gram, across(held[1]), owns, held[1], tiles[2:], panels, rank, flip

time: 88.7 us -> 93.3 us (1.052)
  Pallas kernels: 13.1 us -> 64.1 us
  starting transfers between devices: 51.5 us -> 16.1 us
  waiting for transfers between devices: 22.2 us -> 10.3 us
    pallas_call x4 -> x6, Pallas kernels: 2.62 us -> 47.1 us  [sketch_pass(): pl.pallas_call(functools.partial(sketch_kernel, first=first, panels=panel...]
    ppermute x16 -> x17, starting transfers between devices: 51.5 us -> 16.1 us  [swap(): return lax.ppermute(x, 'tile', [(i, i ^ k) for i in range(n)])]
    ppermute x16 -> x17, waiting for transfers between devices: 22.2 us -> 10.3 us  [swap(): return lax.ppermute(x, 'tile', [(i, i ^ k) for i in range(n)])]
    pallas_call x1, Pallas kernels: 0.83 us -> 4.01 us  [first_pass(): pl.pallas_call(functools.partial(first_kernel, panels=panels, half=len(ev...]
    pallas_call x1, Pallas kernels: 6.97 us -> 9.7 us  [project_pass(): pl.pallas_call(functools.partial(project_kernel, panels=panels, half=len(...]
  transfers between devices with their start and end apart: 16 -> 17, of which waited for: 10 -> 5; matrix products, arithmetic and copies ran while one was open for 0% -> 0% of each run, Pallas kernels for 3% -> 44%
where the time goes in v2:
time: 93.3 us; the launch traced here: 91.4 us
  Pallas kernels  64.1 us (69%)
  starting transfers between devices  16.1 us (17%)
  waiting for transfers between devices  10.3 us (11%)
    pallas_call x6, Pallas kernels, sketch_pass(): pl.pallas_call(functools.partial(sketch_kernel, first=first, panels=panel...  47.1 us
    ppermute x17, starting transfers between devices, swap(): return lax.ppermute(x, 'tile', [(i, i ^ k) for i in range(n)])  16.1 us
    ppermute x17, waiting for transfers between devices, swap(): return lax.ppermute(x, 'tile', [(i, i ^ k) for i in range(n)])  10.3 us
    pallas_call x1, Pallas kernels, project_pass(): pl.pallas_call(functools.partial(project_kernel, panels=panels, half=len(...  9.7 us
    pallas_call x1, Pallas kernels, first_pass(): pl.pallas_call(functools.partial(first_kernel, panels=panels, half=len(ev...  4.01 us
    pallas_call x1, Pallas kernels, prep(): pl.pallas_call(functools.partial(prep_kernel, slices=slices, place=place)...  2.88 us
  transfers between devices with their start and end apart: 17, of which 5 were waited for; matrix products, arithmetic and copies ran while one was open for 0% of the time, Pallas kernels for 44%

profile of v2, /device:TPU:0, one launch (start us, length us, event | category | flops | bytes accessed | tf_op | source)
XLA Modules:
  0.0 91.4 jit_solution(5841396573845872980)
XLA Ops:
  0.6 2.9 %prep.1 = (s32[40]{0:T(128)S(1)}, bf16[32,4096]{1,0:T(8,128)(2,1)S(1)}, bf16[4096,128]{1,0:T(8,128)(2,1)S(1)}, bf16[4096,32]{1,0:T(8,128)(2,1)S(1)}) custom-call(s32[1,32]{1,0:T(1,128)} %flags_hbm.1, f32[3,16384]{1,0:T(4,128)} %rows_hbm.1, f32[3,4096]{1,0:T(4,128)} %src_hbm.1, bf16[4096,128]{1,0:T(8,128)(2,1)} %omega_hbm.1), custom_call_target="tpu_custom_call" | custom-call | tf_op jit(solution)/shard_map/prep/pallas_call | solution.py:165
  3.5 11.5 %sketch_pass.6 = (f32[1024,128]{1,0:T(8,128)S(1)}, bf16[32,1024,128]{2,1,0:T(8,128)(2,1)S(1)}) custom-call(s32[40]{0:T(128)S(1)} %get-tuple-element.58.order_ref, bf16[32,4096]{1,0:T(8,128)(2,1)S(1)} %get-tuple-element.40.src_pick, bf16[4096,128]{1,0:T(8,128)(2,1)S(1)} %get-tuple-element.41.omega_pick, bf16[4096,32]{1,0:T(8,128)(2,1)S(1)} %get-tuple-element.42.row_mat), custom_call_target="tpu_custom_call" | custom-call | flops 8589934592 | bytes 8388608 | tf_op jit(solution)/shard_map/sketch_pass/pallas_call | solution.py:231
  15.0 0.1 collective-permute-start
  15.1 11.5 %sketch_pass.7 = (f32[1024,128]{1,0:T(8,128)S(1)}, bf16[32,1024,128]{2,1,0:T(8,128)(2,1)S(1)}) custom-call(s32[40]{0:T(128)S(1)} %get-tuple-element.58.order_ref, bf16[32,4096]{1,0:T(8,128)(2,1)S(1)} %get-tuple-element.40.src_pick, bf16[4096,128]{1,0:T(8,128)(2,1)S(1)} %get-tuple-element.41.omega_pick, bf16[4096,32]{1,0:T(8,128)(2,1)S(1)} %get-tuple-element.42.row_mat), custom_call_target="tpu_custom_call" | custom-call | flops 8589934592 | bytes 8388608 | tf_op jit(solution)/shard_map/sketch_pass/pallas_call | solution.py:231
  26.6 0.0 collective-permute-done.refs_1_
  26.6 0.1 pair_sum.2
  26.6 3.1 %collective-permute-start.1 = (bf16[256,128]{1,0:T(8,128)(2,1)S(1)}, bf16[256,128]{1,0:T(8,128)(2,1)S(1)}, u32[]{:S(2)}, u32[]{:S(2)}) collective-permute-start(bf16[256,128]{1,0:T(8,128)(2,1)S(1)} %get-tuple-element.52), channel_id=1, source_target_pairs={{0,2},{1,3},{2,0},{3,1},{4,6},{5,7},{6,4},{7,5},{8,10},{9,11},{10,... | collective-permute-start | bytes 196616 | tf_op jit(solution)/shard_map/ppermute | solution.py:495
  29.8 0.0 collective-permute-start.2
  29.8 6.0 %sketch_pass.8 = (f32[512,128]{1,0:T(8,128)S(1)}, bf16[32,512,128]{2,1,0:T(8,128)(2,1)S(1)}) custom-call(s32[40]{0:T(128)S(1)} %get-tuple-element.58.order_ref, bf16[32,4096]{1,0:T(8,128)(2,1)S(1)} %get-tuple-element.40.src_pick, bf16[4096,128]{1,0:T(8,128)(2,1)S(1)} %get-tuple-element.41.omega_pick, bf16[4096,32]{1,0:T(8,128)(2,1)S(1)} %get-tuple-element.42.row_mat), custom_call_target="tpu_custom_call" | custom-call | flops 4294967296 | bytes 4194304 | tf_op jit(solution)/shard_map/sketch_pass/pallas_call | solution.py:231
  35.8 0.1 collective-permute-start.8
  35.9 0.0 collective-permute-done.1.refs_0_
  35.9 0.0 collective-permute-done.2.refs_1_
  35.9 1.8 %collective-permute-start.3 = (bf16[256,128]{1,0:T(8,128)(2,1)S(1)}, bf16[256,128]{1,0:T(8,128)(2,1)S(1)}, u32[]{:S(2)}, u32[]{:S(2)}) collective-permute-start(bf16[256,128]{1,0:T(8,128)(2,1)S(1)} %get-tuple-element.55), channel_id=1, source_target_pairs={{0,6},{1,7},{2,4},{3,5},{4,2},{5,3},{6,0},{7,1},{8,14},{9,15},{10,... | collective-permute-start | bytes 196616 | tf_op jit(solution)/shard_map/ppermute | solution.py:495
  37.7 6.2 %sketch_pass.9 = (f32[512,128]{1,0:T(8,128)S(1)}, bf16[32,512,128]{2,1,0:T(8,128)(2,1)S(1)}) custom-call(s32[40]{0:T(128)S(1)} %get-tuple-element.58.order_ref, bf16[32,4096]{1,0:T(8,128)(2,1)S(1)} %get-tuple-element.40.src_pick, bf16[4096,128]{1,0:T(8,128)(2,1)S(1)} %get-tuple-element.41.omega_pick, bf16[4096,32]{1,0:T(8,128)(2,1)S(1)} %get-tuple-element.42.row_mat), custom_call_target="tpu_custom_call" | custom-call | flops 4294967296 | bytes 4194304 | tf_op jit(solution)/shard_map/sketch_pass/pallas_call | solution.py:231
  43.9 0.1 collective-permute-start.9
  44.0 0.0 collective-permute-done.3.refs_2_
  44.0 0.1 row_sum.2.refs_0_
  44.1 0.1 collective-permute-start.5
  44.2 2.7 %collective-permute-start.4 = (bf16[128,256]{1,0:T(8,128)(2,1)S(1)}, bf16[128,256]{1,0:T(8,128)(2,1)S(1)}, u32[]{:S(2)}, u32[]{:S(2)}) collective-permute-start(bf16[128,256]{1,0:T(8,128)(2,1)S(1)} %row_sum.2.refs_0_), channel_id=1, source_target_pairs={{0,2},{1,3},{2,0},{3,1},{4,6},{5,7},{6,4},{7,5},{8,10},{9,11},{10,... | collective-permute-start | bytes 196616 | tf_op jit(solution)/shard_map/ppermute | solution.py:495
  46.9 6.0 %sketch_pass.10 = (f32[512,128]{1,0:T(8,128)S(1)}, bf16[32,512,128]{2,1,0:T(8,128)(2,1)S(1)}) custom-call(s32[40]{0:T(128)S(1)} %get-tuple-element.58.order_ref, bf16[32,4096]{1,0:T(8,128)(2,1)S(1)} %get-tuple-element.40.src_pick, bf16[4096,128]{1,0:T(8,128)(2,1)S(1)} %get-tuple-element.41.omega_pick, bf16[4096,32]{1,0:T(8,128)(2,1)S(1)} %get-tuple-element.42.row_mat), custom_call_target="tpu_custom_call" | custom-call | flops 4294967296 | bytes 4194304 | tf_op jit(solution)/shard_map/sketch_pass/pallas_call | solution.py:231
  52.9 0.0 collective-permute-done.5.refs_2_
  52.9 0.0 collective-permute-done.4.refs_1_
  52.9 0.1 collective-permute-start.6
  53.0 6.0 %sketch_pass.11 = (f32[512,128]{1,0:T(8,128)S(1)}, bf16[32,512,128]{2,1,0:T(8,128)(2,1)S(1)}) custom-call(s32[40]{0:T(128)S(1)} %get-tuple-element.58.order_ref, bf16[32,4096]{1,0:T(8,128)(2,1)S(1)} %get-tuple-element.40.src_pick, bf16[4096,128]{1,0:T(8,128)(2,1)S(1)} %get-tuple-element.41.omega_pick, bf16[4096,32]{1,0:T(8,128)(2,1)S(1)} %get-tuple-element.42.row_mat), custom_call_target="tpu_custom_call" | custom-call | flops 4294967296 | bytes 4194304 | tf_op jit(solution)/shard_map/sketch_pass/pallas_call | solution.py:231
  59.0 0.0 collective-permute-done.6.refs_3_
  59.1 0.1 collective-permute-start.7
  59.2 0.0 collective-permute-done.8.refs_2_
  59.2 0.0 collective-permute-done.9.refs_3_
  59.2 0.1 pair_sum.3
  59.3 0.1 collective-permute-start.10
  59.3 2.1 %collective-permute-start.11 = (bf16[256,128]{1,0:T(8,128)(2,1)S(1)}, bf16[256,128]{1,0:T(8,128)(2,1)S(1)}, u32[]{:S(2)}, u32[]{:S(2)}) collective-permute-start(bf16[256,128]{1,0:T(8,128)(2,1)S(1)} %get-tuple-element.69), channel_id=1, source_target_pairs={{0,4},{1,5},{2,6},{3,7},{4,0},{5,1},{6,2},{7,3},{8,12},{9,13},{10,... | collective-permute-start | bytes 196616 | tf_op jit(solution)/shard_map/ppermute | solution.py:495
  61.4 0.0 collective-permute-done.7.odd_ref
  61.4 4.0 %first_pass.1 = (f32[128,4096]{1,0:T(8,128)S(1)}, f32[128,128]{1,0:T(8,128)S(1)}) custom-call(s32[40]{0:T(128)S(1)} %get-tuple-element.58.order_ref, bf16[4,128,256]{2,1,0:T(8,128)(2,1)S(1)} %collective-permute-done.7.odd_ref, bf16[128,256]{1,0:T(8,128)(2,1)S(1)} %row_sum.2.refs_0_, bf16[128,256]{1,0:T(8,128)(2,1)S(1)} %collective-permute-done.4.refs_1_, ...), custom_call_target="tpu_custom_call" | custom-call | flops 2147483648 | tf_op jit(solution)/shard_map/first_pass/pallas_call | solution.py:383
  65.4 0.0 collective-permute-done.10.refs_0_
  65.4 0.8 collective-permute-done.11.refs_1_
  66.2 1.3 %collective-permute-start.12 = (bf16[256,128]{1,0:T(8,128)(2,1)S(1)}, bf16[256,128]{1,0:T(8,128)(2,1)S(1)}, u32[]{:S(2)}, u32[]{:S(2)}) collective-permute-start(bf16[256,128]{1,0:T(8,128)(2,1)S(1)} %get-tuple-element.71), channel_id=1, source_target_pairs={{0,6},{1,7},{2,4},{3,5},{4,2},{5,3},{6,0},{7,1},{8,14},{9,15},{10,... | collective-permute-start | bytes 196616 | tf_op jit(solution)/shard_map/ppermute | solution.py:495
  67.6 4.8 %collective-permute-done.12.refs_2_ = bf16[256,128]{1,0:T(8,128)(2,1)S(1)} collective-permute-done((bf16[256,128]{1,0:T(8,128)(2,1)S(1)}, bf16[256,128]{1,0:T(8,128)(2,1)S(1)}, u32[]{:S(2)}, u32[]{:S(2)}) %collective-permute-start.12) | collective-permute-done | bytes 65568 | tf_op jit(solution)/shard_map/ppermute | solution.py:495
  72.4 0.1 row_sum.3.refs_0_.refs_1_.refs_2_
  72.5 1.4 %collective-permute-start.15 = (bf16[128,256]{1,0:T(8,128)(2,1)S(1)}, bf16[128,256]{1,0:T(8,128)(2,1)S(1)}, u32[]{:S(2)}, u32[]{:S(2)}) collective-permute-start(bf16[128,256]{1,0:T(8,128)(2,1)S(1)} %row_sum.3.refs_0_.refs_1_.refs_2_), channel_id=1, source_target_pairs={{0,6},{1,7},{2,4},{3,5},{4,2},{5,3},{6,0},{7,1},{8,14},{9,15},{10,... | collective-permute-start | bytes 196616 | tf_op jit(solution)/shard_map/ppermute | solution.py:495
  73.9 0.0 collective-permute-start.14
  73.9 3.1 %collective-permute-start.13 = (bf16[128,256]{1,0:T(8,128)(2,1)S(1)}, bf16[128,256]{1,0:T(8,128)(2,1)S(1)}, u32[]{:S(2)}, u32[]{:S(2)}) collective-permute-start(bf16[128,256]{1,0:T(8,128)(2,1)S(1)} %row_sum.3.refs_0_.refs_1_.refs_2_), channel_id=1, source_target_pairs={{0,2},{1,3},{2,0},{3,1},{4,6},{5,7},{6,4},{7,5},{8,10},{9,11},{10,... | collective-permute-start | bytes 196616 | tf_op jit(solution)/shard_map/ppermute | solution.py:495
  76.9 1.8 %collective-permute-done.15.refs_3_.refs_5_ = bf16[128,256]{1,0:T(8,128)(2,1)S(1)} collective-permute-done((bf16[128,256]{1,0:T(8,128)(2,1)S(1)}, bf16[128,256]{1,0:T(8,128)(2,1)S(1)}, u32[]{:S(2)}, u32[]{:S(2)}) %collective-permute-start.15) | collective-permute-done | bytes 65568 | tf_op jit(solution)/shard_map/ppermute | solution.py:495
  78.7 1.3 %collective-permute-done.14.refs_2_.refs_4_ = bf16[128,256]{1,0:T(8,128)(2,1)S(1)} collective-permute-done((bf16[128,256]{1,0:T(8,128)(2,1)S(1)}, bf16[128,256]{1,0:T(8,128)(2,1)S(1)}, u32[]{:S(2)}, u32[]{:S(2)}) %collective-permute-start.14) | collective-permute-done | bytes 65568 | tf_op jit(solution)/shard_map/ppermute | solution.py:495
  80.1 0.0 collective-permute-done.13.refs_1_.refs_3_
  80.1 0.1 collective-permute-start.16
  80.2 1.5 %collective-permute-done.16.odd_ref = bf16[4,128,256]{2,1,0:T(8,128)(2,1)S(1)} collective-permute-done((bf16[4,128,256]{2,1,0:T(8,128)(2,1)S(1)}, bf16[4,128,256]{2,1,0:T(8,128)(2,1)S(1)}, u32[]{:S(2)}, u32[]{:S(2)}) %collective-permute-start.16) | collective-permute-done | bytes 262176 | tf_op jit(solution)/shard_map/ppermute | solution.py:495
  81.7 9.7 %project_pass.1 = (f32[512,128]{1,0:T(8,128)}, bf16[1,128,4096]{2,1,0:T(8,128)(2,1)}) custom-call(s32[40]{0:T(128)S(1)} %get-tuple-element.58.order_ref, f32[128,4096]{1,0:T(8,128)S(1)} %get-tuple-element.64.first_ref, f32[128,128]{1,0:T(8,128)S(1)} %get-tuple-element.65.gram_ref, bf16[4,128,256]{2,1,0:T(8,128)(2,1)S(1)} %collective-permute-done.16.odd_ref, ...), custom_call_target="tpu_custom_call" | custom-call | tf_op jit(solution)/shard_map/project_pass/pallas_call | solution.py:457
  (2 shorter events, 0.0 us)
Async XLA Ops:
  15.0 11.6 %collective-permute-start = (f32[1024,128]{1,0:T(8,128)S(1)}, f32[1024,128]{1,0:T(8,128)S(1)}, u32[]{:S(2)}, u32[]{:S(2)}) collective-permute-start(f32[1024,128]{1,0:T(8,128)S(1)} %get-tuple-element.43), channel_id=1, source_target_pairs={{0,1},{1,0},{2,3},{3,2},{4,5},{5,4},{6,7},{7,6},{8,9},{9,8},{10,11... | collective-permute-start | bytes 1572872 | tf_op jit(solution)/shard_map/ppermute | solution.py:495
  26.6 9.2 %collective-permute-start.1 = (bf16[256,128]{1,0:T(8,128)(2,1)S(1)}, bf16[256,128]{1,0:T(8,128)(2,1)S(1)}, u32[]{:S(2)}, u32[]{:S(2)}) collective-permute-start(bf16[256,128]{1,0:T(8,128)(2,1)S(1)} %get-tuple-element.52), channel_id=1, source_target_pairs={{0,2},{1,3},{2,0},{3,1},{4,6},{5,7},{6,4},{7,5},{8,10},{9,11},{10,... | collective-permute-start | bytes 196616 | tf_op jit(solution)/shard_map/ppermute | solution.py:495
  29.8 6.1 %collective-permute-start.2 = (bf16[256,128]{1,0:T(8,128)(2,1)S(1)}, bf16[256,128]{1,0:T(8,128)(2,1)S(1)}, u32[]{:S(2)}, u32[]{:S(2)}) collective-permute-start(bf16[256,128]{1,0:T(8,128)(2,1)S(1)} %get-tuple-element.53), channel_id=1, source_target_pairs={{0,4},{1,5},{2,6},{3,7},{4,0},{5,1},{6,2},{7,3},{8,12},{9,13},{10,... | collective-permute-start | bytes 196616 | tf_op jit(solution)/shard_map/ppermute | solution.py:495
  35.8 23.4 %collective-permute-start.8 = (f32[512,128]{1,0:T(8,128)S(1)}, f32[512,128]{1,0:T(8,128)S(1)}, u32[]{:S(2)}, u32[]{:S(2)}) collective-permute-start(f32[512,128]{1,0:T(8,128)S(1)} %get-tuple-element.48), channel_id=1, source_target_pairs={{0,1},{1,0},{2,3},{3,2},{4,5},{5,4},{6,7},{7,6},{8,9},{9,8},{10,11... | collective-permute-start | bytes 786440 | tf_op jit(solution)/shard_map/ppermute | solution.py:495
  35.9 8.1 %collective-permute-start.3 = (bf16[256,128]{1,0:T(8,128)(2,1)S(1)}, bf16[256,128]{1,0:T(8,128)(2,1)S(1)}, u32[]{:S(2)}, u32[]{:S(2)}) collective-permute-start(bf16[256,128]{1,0:T(8,128)(2,1)S(1)} %get-tuple-element.55), channel_id=1, source_target_pairs={{0,6},{1,7},{2,4},{3,5},{4,2},{5,3},{6,0},{7,1},{8,14},{9,15},{10,... | collective-permute-start | bytes 196616 | tf_op jit(solution)/shard_map/ppermute | solution.py:495
  43.9 15.3 %collective-permute-start.9 = (f32[512,128]{1,0:T(8,128)S(1)}, f32[512,128]{1,0:T(8,128)S(1)}, u32[]{:S(2)}, u32[]{:S(2)}) collective-permute-start(f32[512,128]{1,0:T(8,128)S(1)} %get-tuple-element.50), channel_id=1, source_target_pairs={{0,1},{1,0},{2,3},{3,2},{4,5},{5,4},{6,7},{7,6},{8,9},{9,8},{10,11... | collective-permute-start | bytes 786440 | tf_op jit(solution)/shard_map/ppermute | solution.py:495
  44.1 8.8 %collective-permute-start.5 = (bf16[128,256]{1,0:T(8,128)(2,1)S(1)}, bf16[128,256]{1,0:T(8,128)(2,1)S(1)}, u32[]{:S(2)}, u32[]{:S(2)}) collective-permute-start(bf16[128,256]{1,0:T(8,128)(2,1)S(1)} %row_sum.2.refs_0_), channel_id=1, source_target_pairs={{0,4},{1,5},{2,6},{3,7},{4,0},{5,1},{6,2},{7,3},{8,12},{9,13},{10,... | collective-permute-start | bytes 196616 | tf_op jit(solution)/shard_map/ppermute | solution.py:495
  44.2 8.8 %collective-permute-start.4 = (bf16[128,256]{1,0:T(8,128)(2,1)S(1)}, bf16[128,256]{1,0:T(8,128)(2,1)S(1)}, u32[]{:S(2)}, u32[]{:S(2)}) collective-permute-start(bf16[128,256]{1,0:T(8,128)(2,1)S(1)} %row_sum.2.refs_0_), channel_id=1, source_target_pairs={{0,2},{1,3},{2,0},{3,1},{4,6},{5,7},{6,4},{7,5},{8,10},{9,11},{10,... | collective-permute-start | bytes 196616 | tf_op jit(solution)/shard_map/ppermute | solution.py:495
  52.9 6.1 %collective-permute-start.6 = (bf16[128,256]{1,0:T(8,128)(2,1)S(1)}, bf16[128,256]{1,0:T(8,128)(2,1)S(1)}, u32[]{:S(2)}, u32[]{:S(2)}) collective-permute-start(bf16[128,256]{1,0:T(8,128)(2,1)S(1)} %row_sum.2.refs_0_), channel_id=1, source_target_pairs={{0,6},{1,7},{2,4},{3,5},{4,2},{5,3},{6,0},{7,1},{8,14},{9,15},{10,... | collective-permute-start | bytes 196616 | tf_op jit(solution)/shard_map/ppermute | solution.py:495
  59.1 2.3 %collective-permute-start.7 = (bf16[4,128,256]{2,1,0:T(8,128)(2,1)S(1)}, bf16[4,128,256]{2,1,0:T(8,128)(2,1)S(1)}, u32[]{:S(2)}, u32[]{:S(2)}) collective-permute-start(bf16[4,128,256]{2,1,0:T(8,128)(2,1)S(1)} %join.2), channel_id=1, source_target_pairs={{0,1},{1,0},{2,3},{3,2},{4,5},{5,4},{6,7},{7,6},{8,9},{9,8},{10,11... | collective-permute-start | bytes 786440 | tf_op jit(solution)/shard_map/ppermute | solution.py:495
  59.3 6.2 %collective-permute-start.10 = (bf16[256,128]{1,0:T(8,128)(2,1)S(1)}, bf16[256,128]{1,0:T(8,128)(2,1)S(1)}, u32[]{:S(2)}, u32[]{:S(2)}) collective-permute-start(bf16[256,128]{1,0:T(8,128)(2,1)S(1)} %get-tuple-element.68), channel_id=1, source_target_pairs={{0,2},{1,3},{2,0},{3,1},{4,6},{5,7},{6,4},{7,5},{8,10},{9,11},{10,... | collective-permute-start | bytes 196616 | tf_op jit(solution)/shard_map/ppermute | solution.py:495
  59.3 6.9 %collective-permute-start.11 = (bf16[256,128]{1,0:T(8,128)(2,1)S(1)}, bf16[256,128]{1,0:T(8,128)(2,1)S(1)}, u32[]{:S(2)}, u32[]{:S(2)}) collective-permute-start(bf16[256,128]{1,0:T(8,128)(2,1)S(1)} %get-tuple-element.69), channel_id=1, source_target_pairs={{0,4},{1,5},{2,6},{3,7},{4,0},{5,1},{6,2},{7,3},{8,12},{9,13},{10,... | collective-permute-start | bytes 196616 | tf_op jit(solution)/shard_map/ppermute | solution.py:495
  66.2 6.2 %collective-permute-start.12 = (bf16[256,128]{1,0:T(8,128)(2,1)S(1)}, bf16[256,128]{1,0:T(8,128)(2,1)S(1)}, u32[]{:S(2)}, u32[]{:S(2)}) collective-permute-start(bf16[256,128]{1,0:T(8,128)(2,1)S(1)} %get-tuple-element.71), channel_id=1, source_target_pairs={{0,6},{1,7},{2,4},{3,5},{4,2},{5,3},{6,0},{7,1},{8,14},{9,15},{10,... | collective-permute-start | bytes 196616 | tf_op jit(solution)/shard_map/ppermute | solution.py:495
  72.5 6.2 %collective-permute-start.15 = (bf16[128,256]{1,0:T(8,128)(2,1)S(1)}, bf16[128,256]{1,0:T(8,128)(2,1)S(1)}, u32[]{:S(2)}, u32[]{:S(2)}) collective-permute-start(bf16[128,256]{1,0:T(8,128)(2,1)S(1)} %row_sum.3.refs_0_.refs_1_.refs_2_), channel_id=1, source_target_pairs={{0,6},{1,7},{2,4},{3,5},{4,2},{5,3},{6,0},{7,1},{8,14},{9,15},{10,... | collective-permute-start | bytes 196616 | tf_op jit(solution)/shard_map/ppermute | solution.py:495
  73.9 6.2 %collective-permute-start.14 = (bf16[128,256]{1,0:T(8,128)(2,1)S(1)}, bf16[128,256]{1,0:T(8,128)(2,1)S(1)}, u32[]{:S(2)}, u32[]{:S(2)}) collective-permute-start(bf16[128,256]{1,0:T(8,128)(2,1)S(1)} %row_sum.3.refs_0_.refs_1_.refs_2_), channel_id=1, source_target_pairs={{0,4},{1,5},{2,6},{3,7},{4,0},{5,1},{6,2},{7,3},{8,12},{9,13},{10,... | collective-permute-start | bytes 196616 | tf_op jit(solution)/shard_map/ppermute | solution.py:495
  73.9 6.2 %collective-permute-start.13 = (bf16[128,256]{1,0:T(8,128)(2,1)S(1)}, bf16[128,256]{1,0:T(8,128)(2,1)S(1)}, u32[]{:S(2)}, u32[]{:S(2)}) collective-permute-start(bf16[128,256]{1,0:T(8,128)(2,1)S(1)} %row_sum.3.refs_0_.refs_1_.refs_2_), channel_id=1, source_target_pairs={{0,2},{1,3},{2,0},{3,1},{4,6},{5,7},{6,4},{7,5},{8,10},{9,11},{10,... | collective-permute-start | bytes 196616 | tf_op jit(solution)/shard_map/ppermute | solution.py:495
  80.1 1.6 %collective-permute-start.16 = (bf16[4,128,256]{2,1,0:T(8,128)(2,1)S(1)}, bf16[4,128,256]{2,1,0:T(8,128)(2,1)S(1)}, u32[]{:S(2)}, u32[]{:S(2)}) collective-permute-start(bf16[4,128,256]{2,1,0:T(8,128)(2,1)S(1)} %join.3), channel_id=1, source_target_pairs={{0,1},{1,0},{2,3},{3,2},{4,5},{5,4},{6,7},{7,6},{8,9},{9,8},{10,11... | collective-permute-start | bytes 786440 | tf_op jit(solution)/shard_map/ppermute | solution.py:495

commit v3 on v2

--- a/solution.py
+++ b/solution.py
@@ -559,8 +559,8 @@
 
     odd = across(held[0], own_b)
     first, gram = first_pass(order, odd, held[0], tiles[:2], panels, rank, flip)
-    got_z = z_swaps(sent, gram)
-    held.append(along_z(row_sum(kept, got_z, flip)))
+    got_z = z_swaps(sent)
+    held.append(along_z(row_sum(after(kept, gram), got_z, flip)))
     owns = [h[0] for h in held]
     return project_pass(
         order, first, gram, across(held[1]), owns, held[1], tiles[2:], panels, rank, flip

time: 93.3 us -> 86.8 us (0.930)
  the two profiles are of different devices: /device:TPU:0 before, /device:TPU:3 now
where the time goes in v3:
time: 86.8 us; the launch traced here: 87.8 us
  Pallas kernels  62.2 us (72%)
  starting transfers between devices  16.9 us (19%)
  waiting for transfers between devices  7.79 us (9%)
  between operations  0.89 us (1%)
    pallas_call x6, Pallas kernels, sketch_pass(): pl.pallas_call(functools.partial(sketch_kernel, first=first, panels=panel...  47.1 us
    ppermute x17, starting transfers between devices, swap(): return lax.ppermute(x, 'tile', [(i, i ^ k) for i in range(n)])  16.9 us
    pallas_call x1, Pallas kernels, project_pass(): pl.pallas_call(functools.partial(project_kernel, panels=panels, half=len(...  8.91 us
    ppermute x17, waiting for transfers between devices, swap(): return lax.ppermute(x, 'tile', [(i, i ^ k) for i in range(n)])  7.79 us
    pallas_call x1, Pallas kernels, first_pass(): pl.pallas_call(functools.partial(first_kernel, panels=panels, half=len(ev...  3.1 us
    pallas_call x1, Pallas kernels, prep(): pl.pallas_call(functools.partial(prep_kernel, slices=slices, place=place)...  2.75 us
  transfers between devices with their start and end apart: 17, of which 4 were waited for; matrix products, arithmetic and copies ran while one was open for 0% of the time, Pallas kernels for 44%

profile of v3, /device:TPU:3, one launch (start us, length us, event | category | flops | bytes accessed | tf_op | source)
XLA Modules:
  0.0 87.8 jit_solution(6123488447505803479)
XLA Ops:
  0.6 2.8 %prep.1 = (s32[40]{0:T(128)S(1)}, bf16[32,4096]{1,0:T(8,128)(2,1)S(1)}, bf16[4096,128]{1,0:T(8,128)(2,1)S(1)}, bf16[4096,32]{1,0:T(8,128)(2,1)S(1)}) custom-call(s32[1,32]{1,0:T(1,128)} %flags_hbm.1, f32[3,16384]{1,0:T(4,128)} %rows_hbm.1, f32[3,4096]{1,0:T(4,128)} %src_hbm.1, bf16[4096,128]{1,0:T(8,128)(2,1)} %omega_hbm.1), custom_call_target="tpu_custom_call" | custom-call | tf_op jit(solution)/shard_map/prep/pallas_call | solution.py:165
  3.4 11.5 %sketch_pass.6 = (f32[1024,128]{1,0:T(8,128)S(1)}, bf16[32,1024,128]{2,1,0:T(8,128)(2,1)S(1)}) custom-call(s32[40]{0:T(128)S(1)} %get-tuple-element.58.order_ref, bf16[32,4096]{1,0:T(8,128)(2,1)S(1)} %get-tuple-element.40.src_pick, bf16[4096,128]{1,0:T(8,128)(2,1)S(1)} %get-tuple-element.41.omega_pick, bf16[4096,32]{1,0:T(8,128)(2,1)S(1)} %get-tuple-element.42.row_mat), custom_call_target="tpu_custom_call" | custom-call | flops 8589934592 | bytes 8388608 | tf_op jit(solution)/shard_map/sketch_pass/pallas_call | solution.py:231
  14.9 0.1 collective-permute-start
  14.9 11.5 %sketch_pass.7 = (f32[1024,128]{1,0:T(8,128)S(1)}, bf16[32,1024,128]{2,1,0:T(8,128)(2,1)S(1)}) custom-call(s32[40]{0:T(128)S(1)} %get-tuple-element.58.order_ref, bf16[32,4096]{1,0:T(8,128)(2,1)S(1)} %get-tuple-element.40.src_pick, bf16[4096,128]{1,0:T(8,128)(2,1)S(1)} %get-tuple-element.41.omega_pick, bf16[4096,32]{1,0:T(8,128)(2,1)S(1)} %get-tuple-element.42.row_mat), custom_call_target="tpu_custom_call" | custom-call | flops 8589934592 | bytes 8388608 | tf_op jit(solution)/shard_map/sketch_pass/pallas_call | solution.py:231
  26.4 0.0 collective-permute-done.refs_1_
  26.4 0.1 pair_sum.2
  26.5 0.1 collective-permute-start.1
  26.6 3.8 %collective-permute-start.2 = (bf16[256,128]{1,0:T(8,128)(2,1)S(1)}, bf16[256,128]{1,0:T(8,128)(2,1)S(1)}, u32[]{:S(2)}, u32[]{:S(2)}) collective-permute-start(bf16[256,128]{1,0:T(8,128)(2,1)S(1)} %get-tuple-element.53), channel_id=1, source_target_pairs={{0,4},{1,5},{2,6},{3,7},{4,0},{5,1},{6,2},{7,3},{8,12},{9,13},{10,... | collective-permute-start | bytes 196616 | tf_op jit(solution)/shard_map/ppermute | solution.py:495
  30.4 6.0 %sketch_pass.8 = (f32[512,128]{1,0:T(8,128)S(1)}, bf16[32,512,128]{2,1,0:T(8,128)(2,1)S(1)}) custom-call(s32[40]{0:T(128)S(1)} %get-tuple-element.58.order_ref, bf16[32,4096]{1,0:T(8,128)(2,1)S(1)} %get-tuple-element.40.src_pick, bf16[4096,128]{1,0:T(8,128)(2,1)S(1)} %get-tuple-element.41.omega_pick, bf16[4096,32]{1,0:T(8,128)(2,1)S(1)} %get-tuple-element.42.row_mat), custom_call_target="tpu_custom_call" | custom-call | flops 4294967296 | bytes 4194304 | tf_op jit(solution)/shard_map/sketch_pass/pallas_call | solution.py:231
  36.4 0.1 collective-permute-start.8
  36.4 0.0 collective-permute-done.1.refs_0_
  36.5 0.0 collective-permute-done.2.refs_1_
  36.5 0.1 collective-permute-start.3
  36.5 6.2 %sketch_pass.9 = (f32[512,128]{1,0:T(8,128)S(1)}, bf16[32,512,128]{2,1,0:T(8,128)(2,1)S(1)}) custom-call(s32[40]{0:T(128)S(1)} %get-tuple-element.58.order_ref, bf16[32,4096]{1,0:T(8,128)(2,1)S(1)} %get-tuple-element.40.src_pick, bf16[4096,128]{1,0:T(8,128)(2,1)S(1)} %get-tuple-element.41.omega_pick, bf16[4096,32]{1,0:T(8,128)(2,1)S(1)} %get-tuple-element.42.row_mat), custom_call_target="tpu_custom_call" | custom-call | flops 4294967296 | bytes 4194304 | tf_op jit(solution)/shard_map/sketch_pass/pallas_call | solution.py:231
  42.7 0.1 collective-permute-start.9
  42.8 0.0 collective-permute-done.3.refs_2_
  42.8 0.1 row_sum.2.refs_0_
  42.9 0.1 collective-permute-start.5
  43.0 3.5 %collective-permute-start.4 = (bf16[128,256]{1,0:T(8,128)(2,1)S(1)}, bf16[128,256]{1,0:T(8,128)(2,1)S(1)}, u32[]{:S(2)}, u32[]{:S(2)}) collective-permute-start(bf16[128,256]{1,0:T(8,128)(2,1)S(1)} %row_sum.2.refs_0_), channel_id=1, source_target_pairs={{0,2},{1,3},{2,0},{3,1},{4,6},{5,7},{6,4},{7,5},{8,10},{9,11},{10,... | collective-permute-start | bytes 196616 | tf_op jit(solution)/shard_map/ppermute | solution.py:495
  46.5 6.0 %sketch_pass.10 = (f32[512,128]{1,0:T(8,128)S(1)}, bf16[32,512,128]{2,1,0:T(8,128)(2,1)S(1)}) custom-call(s32[40]{0:T(128)S(1)} %get-tuple-element.58.order_ref, bf16[32,4096]{1,0:T(8,128)(2,1)S(1)} %get-tuple-element.40.src_pick, bf16[4096,128]{1,0:T(8,128)(2,1)S(1)} %get-tuple-element.41.omega_pick, bf16[4096,32]{1,0:T(8,128)(2,1)S(1)} %get-tuple-element.42.row_mat), custom_call_target="tpu_custom_call" | custom-call | flops 4294967296 | bytes 4194304 | tf_op jit(solution)/shard_map/sketch_pass/pallas_call | solution.py:231
  52.5 0.0 collective-permute-done.5.refs_2_
  52.5 0.0 collective-permute-done.4.refs_1_
  52.6 0.1 collective-permute-start.6
  52.6 6.0 %sketch_pass.11 = (f32[512,128]{1,0:T(8,128)S(1)}, bf16[32,512,128]{2,1,0:T(8,128)(2,1)S(1)}) custom-call(s32[40]{0:T(128)S(1)} %get-tuple-element.58.order_ref, bf16[32,4096]{1,0:T(8,128)(2,1)S(1)} %get-tuple-element.40.src_pick, bf16[4096,128]{1,0:T(8,128)(2,1)S(1)} %get-tuple-element.41.omega_pick, bf16[4096,32]{1,0:T(8,128)(2,1)S(1)} %get-tuple-element.42.row_mat), custom_call_target="tpu_custom_call" | custom-call | flops 4294967296 | bytes 4194304 | tf_op jit(solution)/shard_map/sketch_pass/pallas_call | solution.py:231
  58.6 0.0 collective-permute-done.6.refs_3_
  58.7 0.1 collective-permute-start.7
  58.8 0.0 collective-permute-done.8.refs_2_
  58.8 0.0 collective-permute-done.9.refs_3_
  58.8 0.1 pair_sum.3
  58.8 0.1 collective-permute-start.10
  58.9 3.5 %collective-permute-start.11 = (bf16[256,128]{1,0:T(8,128)(2,1)S(1)}, bf16[256,128]{1,0:T(8,128)(2,1)S(1)}, u32[]{:S(2)}, u32[]{:S(2)}) collective-permute-start(bf16[256,128]{1,0:T(8,128)(2,1)S(1)} %get-tuple-element.70), channel_id=1, source_target_pairs={{0,4},{1,5},{2,6},{3,7},{4,0},{5,1},{6,2},{7,3},{8,12},{9,13},{10,... | collective-permute-start | bytes 196616 | tf_op jit(solution)/shard_map/ppermute | solution.py:495
  62.4 0.0 collective-permute-start.12
  62.5 0.0 collective-permute-done.7.odd_ref
  62.5 3.1 %first_pass.1 = (f32[128,4096]{1,0:T(8,128)S(1)}, f32[128,128]{1,0:T(8,128)S(1)}) custom-call(s32[40]{0:T(128)S(1)} %get-tuple-element.58.order_ref, bf16[4,128,256]{2,1,0:T(8,128)(2,1)S(1)} %collective-permute-done.7.odd_ref, bf16[128,256]{1,0:T(8,128)(2,1)S(1)} %row_sum.2.refs_0_, bf16[128,256]{1,0:T(8,128)(2,1)S(1)} %collective-permute-done.4.refs_1_, ...), custom_call_target="tpu_custom_call" | custom-call | flops 2147483648 | tf_op jit(solution)/shard_map/first_pass/pallas_call | solution.py:383
  65.6 0.0 collective-permute-done.10.refs_0_
  65.6 0.0 collective-permute-done.11.refs_1_
  65.6 1.9 %collective-permute-done.12.refs_2_ = bf16[256,128]{1,0:T(8,128)(2,1)S(1)} collective-permute-done((bf16[256,128]{1,0:T(8,128)(2,1)S(1)}, bf16[256,128]{1,0:T(8,128)(2,1)S(1)}, u32[]{:S(2)}, u32[]{:S(2)}) %collective-permute-start.12) | collective-permute-done | bytes 65568 | tf_op jit(solution)/shard_map/ppermute | solution.py:495
  67.4 0.1 row_sum.3.refs_0_.refs_1_.refs_2_
  67.6 2.8 %collective-permute-start.15 = (bf16[128,256]{1,0:T(8,128)(2,1)S(1)}, bf16[128,256]{1,0:T(8,128)(2,1)S(1)}, u32[]{:S(2)}, u32[]{:S(2)}) collective-permute-start(bf16[128,256]{1,0:T(8,128)(2,1)S(1)} %row_sum.3.refs_0_.refs_1_.refs_2_), channel_id=1, source_target_pairs={{0,6},{1,7},{2,4},{3,5},{4,2},{5,3},{6,0},{7,1},{8,14},{9,15},{10,... | collective-permute-start | bytes 196616 | tf_op jit(solution)/shard_map/ppermute | solution.py:495
  70.4 0.0 collective-permute-start.14
  70.4 0.8 collective-permute-start.13
  71.2 1.4 %collective-permute-done.15.refs_3_.refs_5_ = bf16[128,256]{1,0:T(8,128)(2,1)S(1)} collective-permute-done((bf16[128,256]{1,0:T(8,128)(2,1)S(1)}, bf16[128,256]{1,0:T(8,128)(2,1)S(1)}, u32[]{:S(2)}, u32[]{:S(2)}) %collective-permute-start.15) | collective-permute-done | bytes 65568 | tf_op jit(solution)/shard_map/ppermute | solution.py:495
  72.5 3.4 %collective-permute-done.14.refs_2_.refs_4_ = bf16[128,256]{1,0:T(8,128)(2,1)S(1)} collective-permute-done((bf16[128,256]{1,0:T(8,128)(2,1)S(1)}, bf16[128,256]{1,0:T(8,128)(2,1)S(1)}, u32[]{:S(2)}, u32[]{:S(2)}) %collective-permute-start.14) | collective-permute-done | bytes 65568 | tf_op jit(solution)/shard_map/ppermute | solution.py:495
  75.9 0.0 collective-permute-done.13.refs_1_.refs_3_
  75.9 1.8 %collective-permute-start.16 = (bf16[4,128,256]{2,1,0:T(8,128)(2,1)S(1)}, bf16[4,128,256]{2,1,0:T(8,128)(2,1)S(1)}, u32[]{:S(2)}, u32[]{:S(2)}) collective-permute-start(bf16[4,128,256]{2,1,0:T(8,128)(2,1)S(1)} %join.3), channel_id=1, source_target_pairs={{0,1},{1,0},{2,3},{3,2},{4,5},{5,4},{6,7},{7,6},{8,9},{9,8},{10,11... | collective-permute-start | bytes 786440 | tf_op jit(solution)/shard_map/ppermute | solution.py:495
  77.8 1.2 %collective-permute-done.16.odd_ref = bf16[4,128,256]{2,1,0:T(8,128)(2,1)S(1)} collective-permute-done((bf16[4,128,256]{2,1,0:T(8,128)(2,1)S(1)}, bf16[4,128,256]{2,1,0:T(8,128)(2,1)S(1)}, u32[]{:S(2)}, u32[]{:S(2)}) %collective-permute-start.16) | collective-permute-done | bytes 262176 | tf_op jit(solution)/shard_map/ppermute | solution.py:495
  78.9 8.9 %project_pass.1 = (f32[512,128]{1,0:T(8,128)}, bf16[1,128,4096]{2,1,0:T(8,128)(2,1)}) custom-call(s32[40]{0:T(128)S(1)} %get-tuple-element.58.order_ref, f32[128,4096]{1,0:T(8,128)S(1)} %get-tuple-element.64.first_ref, f32[128,128]{1,0:T(8,128)S(1)} %get-tuple-element.65.gram_ref, bf16[4,128,256]{2,1,0:T(8,128)(2,1)S(1)} %collective-permute-done.16.odd_ref, ...), custom_call_target="tpu_custom_call" | custom-call | tf_op jit(solution)/shard_map/project_pass/pallas_call | solution.py:457
  (2 shorter events, 0.0 us)
Async XLA Ops:
  14.9 11.6 %collective-permute-start = (f32[1024,128]{1,0:T(8,128)S(1)}, f32[1024,128]{1,0:T(8,128)S(1)}, u32[]{:S(2)}, u32[]{:S(2)}) collective-permute-start(f32[1024,128]{1,0:T(8,128)S(1)} %get-tuple-element.43), channel_id=1, source_target_pairs={{0,1},{1,0},{2,3},{3,2},{4,5},{5,4},{6,7},{7,6},{8,9},{9,8},{10,11... | collective-permute-start | bytes 1572872 | tf_op jit(solution)/shard_map/ppermute | solution.py:495
  26.5 9.9 %collective-permute-start.1 = (bf16[256,128]{1,0:T(8,128)(2,1)S(1)}, bf16[256,128]{1,0:T(8,128)(2,1)S(1)}, u32[]{:S(2)}, u32[]{:S(2)}) collective-permute-start(bf16[256,128]{1,0:T(8,128)(2,1)S(1)} %get-tuple-element.52), channel_id=1, source_target_pairs={{0,2},{1,3},{2,0},{3,1},{4,6},{5,7},{6,4},{7,5},{8,10},{9,11},{10,... | collective-permute-start | bytes 196616 | tf_op jit(solution)/shard_map/ppermute | solution.py:495
  26.6 9.9 %collective-permute-start.2 = (bf16[256,128]{1,0:T(8,128)(2,1)S(1)}, bf16[256,128]{1,0:T(8,128)(2,1)S(1)}, u32[]{:S(2)}, u32[]{:S(2)}) collective-permute-start(bf16[256,128]{1,0:T(8,128)(2,1)S(1)} %get-tuple-element.53), channel_id=1, source_target_pairs={{0,4},{1,5},{2,6},{3,7},{4,0},{5,1},{6,2},{7,3},{8,12},{9,13},{10,... | collective-permute-start | bytes 196616 | tf_op jit(solution)/shard_map/ppermute | solution.py:495
  36.4 22.4 %collective-permute-start.8 = (f32[512,128]{1,0:T(8,128)S(1)}, f32[512,128]{1,0:T(8,128)S(1)}, u32[]{:S(2)}, u32[]{:S(2)}) collective-permute-start(f32[512,128]{1,0:T(8,128)S(1)} %get-tuple-element.48), channel_id=1, source_target_pairs={{0,1},{1,0},{2,3},{3,2},{4,5},{5,4},{6,7},{7,6},{8,9},{9,8},{10,11... | collective-permute-start | bytes 786440 | tf_op jit(solution)/shard_map/ppermute | solution.py:495
  36.5 6.3 %collective-permute-start.3 = (bf16[256,128]{1,0:T(8,128)(2,1)S(1)}, bf16[256,128]{1,0:T(8,128)(2,1)S(1)}, u32[]{:S(2)}, u32[]{:S(2)}) collective-permute-start(bf16[256,128]{1,0:T(8,128)(2,1)S(1)} %get-tuple-element.55), channel_id=1, source_target_pairs={{0,6},{1,7},{2,4},{3,5},{4,2},{5,3},{6,0},{7,1},{8,14},{9,15},{10,... | collective-permute-start | bytes 196616 | tf_op jit(solution)/shard_map/ppermute | solution.py:495
  42.7 16.0 %collective-permute-start.9 = (f32[512,128]{1,0:T(8,128)S(1)}, f32[512,128]{1,0:T(8,128)S(1)}, u32[]{:S(2)}, u32[]{:S(2)}) collective-permute-start(f32[512,128]{1,0:T(8,128)S(1)} %get-tuple-element.50), channel_id=1, source_target_pairs={{0,1},{1,0},{2,3},{3,2},{4,5},{5,4},{6,7},{7,6},{8,9},{9,8},{10,11... | collective-permute-start | bytes 786440 | tf_op jit(solution)/shard_map/ppermute | solution.py:495
  42.9 9.6 %collective-permute-start.5 = (bf16[128,256]{1,0:T(8,128)(2,1)S(1)}, bf16[128,256]{1,0:T(8,128)(2,1)S(1)}, u32[]{:S(2)}, u32[]{:S(2)}) collective-permute-start(bf16[128,256]{1,0:T(8,128)(2,1)S(1)} %row_sum.2.refs_0_), channel_id=1, source_target_pairs={{0,4},{1,5},{2,6},{3,7},{4,0},{5,1},{6,2},{7,3},{8,12},{9,13},{10,... | collective-permute-start | bytes 196616 | tf_op jit(solution)/shard_map/ppermute | solution.py:495
  43.0 9.5 %collective-permute-start.4 = (bf16[128,256]{1,0:T(8,128)(2,1)S(1)}, bf16[128,256]{1,0:T(8,128)(2,1)S(1)}, u32[]{:S(2)}, u32[]{:S(2)}) collective-permute-start(bf16[128,256]{1,0:T(8,128)(2,1)S(1)} %row_sum.2.refs_0_), channel_id=1, source_target_pairs={{0,2},{1,3},{2,0},{3,1},{4,6},{5,7},{6,4},{7,5},{8,10},{9,11},{10,... | collective-permute-start | bytes 196616 | tf_op jit(solution)/shard_map/ppermute | solution.py:495
  52.6 6.1 %collective-permute-start.6 = (bf16[128,256]{1,0:T(8,128)(2,1)S(1)}, bf16[128,256]{1,0:T(8,128)(2,1)S(1)}, u32[]{:S(2)}, u32[]{:S(2)}) collective-permute-start(bf16[128,256]{1,0:T(8,128)(2,1)S(1)} %row_sum.2.refs_0_), channel_id=1, source_target_pairs={{0,6},{1,7},{2,4},{3,5},{4,2},{5,3},{6,0},{7,1},{8,14},{9,15},{10,... | collective-permute-start | bytes 196616 | tf_op jit(solution)/shard_map/ppermute | solution.py:495
  58.7 3.8 %collective-permute-start.7 = (bf16[4,128,256]{2,1,0:T(8,128)(2,1)S(1)}, bf16[4,128,256]{2,1,0:T(8,128)(2,1)S(1)}, u32[]{:S(2)}, u32[]{:S(2)}) collective-permute-start(bf16[4,128,256]{2,1,0:T(8,128)(2,1)S(1)} %join.2), channel_id=1, source_target_pairs={{0,1},{1,0},{2,3},{3,2},{4,5},{5,4},{6,7},{7,6},{8,9},{9,8},{10,11... | collective-permute-start | bytes 786440 | tf_op jit(solution)/shard_map/ppermute | solution.py:495
  58.8 6.7 %collective-permute-start.10 = (bf16[256,128]{1,0:T(8,128)(2,1)S(1)}, bf16[256,128]{1,0:T(8,128)(2,1)S(1)}, u32[]{:S(2)}, u32[]{:S(2)}) collective-permute-start(bf16[256,128]{1,0:T(8,128)(2,1)S(1)} %get-tuple-element.69), channel_id=1, source_target_pairs={{0,2},{1,3},{2,0},{3,1},{4,6},{5,7},{6,4},{7,5},{8,10},{9,11},{10,... | collective-permute-start | bytes 196616 | tf_op jit(solution)/shard_map/ppermute | solution.py:495
  58.9 6.7 %collective-permute-start.11 = (bf16[256,128]{1,0:T(8,128)(2,1)S(1)}, bf16[256,128]{1,0:T(8,128)(2,1)S(1)}, u32[]{:S(2)}, u32[]{:S(2)}) collective-permute-start(bf16[256,128]{1,0:T(8,128)(2,1)S(1)} %get-tuple-element.70), channel_id=1, source_target_pairs={{0,4},{1,5},{2,6},{3,7},{4,0},{5,1},{6,2},{7,3},{8,12},{9,13},{10,... | collective-permute-start | bytes 196616 | tf_op jit(solution)/shard_map/ppermute | solution.py:495
  62.4 5.0 %collective-permute-start.12 = (bf16[256,128]{1,0:T(8,128)(2,1)S(1)}, bf16[256,128]{1,0:T(8,128)(2,1)S(1)}, u32[]{:S(2)}, u32[]{:S(2)}) collective-permute-start(bf16[256,128]{1,0:T(8,128)(2,1)S(1)} %get-tuple-element.71), channel_id=1, source_target_pairs={{0,6},{1,7},{2,4},{3,5},{4,2},{5,3},{6,0},{7,1},{8,14},{9,15},{10,... | collective-permute-start | bytes 196616 | tf_op jit(solution)/shard_map/ppermute | solution.py:495
  67.6 5.0 %collective-permute-start.15 = (bf16[128,256]{1,0:T(8,128)(2,1)S(1)}, bf16[128,256]{1,0:T(8,128)(2,1)S(1)}, u32[]{:S(2)}, u32[]{:S(2)}) collective-permute-start(bf16[128,256]{1,0:T(8,128)(2,1)S(1)} %row_sum.3.refs_0_.refs_1_.refs_2_), channel_id=1, source_target_pairs={{0,6},{1,7},{2,4},{3,5},{4,2},{5,3},{6,0},{7,1},{8,14},{9,15},{10,... | collective-permute-start | bytes 196616 | tf_op jit(solution)/shard_map/ppermute | solution.py:495
  70.4 5.5 %collective-permute-start.14 = (bf16[128,256]{1,0:T(8,128)(2,1)S(1)}, bf16[128,256]{1,0:T(8,128)(2,1)S(1)}, u32[]{:S(2)}, u32[]{:S(2)}) collective-permute-start(bf16[128,256]{1,0:T(8,128)(2,1)S(1)} %row_sum.3.refs_0_.refs_1_.refs_2_), channel_id=1, source_target_pairs={{0,4},{1,5},{2,6},{3,7},{4,0},{5,1},{6,2},{7,3},{8,12},{9,13},{10,... | collective-permute-start | bytes 196616 | tf_op jit(solution)/shard_map/ppermute | solution.py:495
  70.4 5.5 %collective-permute-start.13 = (bf16[128,256]{1,0:T(8,128)(2,1)S(1)}, bf16[128,256]{1,0:T(8,128)(2,1)S(1)}, u32[]{:S(2)}, u32[]{:S(2)}) collective-permute-start(bf16[128,256]{1,0:T(8,128)(2,1)S(1)} %row_sum.3.refs_0_.refs_1_.refs_2_), channel_id=1, source_target_pairs={{0,2},{1,3},{2,0},{3,1},{4,6},{5,7},{6,4},{7,5},{8,10},{9,11},{10,... | collective-permute-start | bytes 196616 | tf_op jit(solution)/shard_map/ppermute | solution.py:495
  75.9 3.0 %collective-permute-start.16 = (bf16[4,128,256]{2,1,0:T(8,128)(2,1)S(1)}, bf16[4,128,256]{2,1,0:T(8,128)(2,1)S(1)}, u32[]{:S(2)}, u32[]{:S(2)}) collective-permute-start(bf16[4,128,256]{2,1,0:T(8,128)(2,1)S(1)} %join.3), channel_id=1, source_target_pairs={{0,1},{1,0},{2,3},{3,2},{4,5},{5,4},{6,7},{7,6},{8,9},{9,8},{10,11... | collective-permute-start | bytes 786440 | tf_op jit(solution)/shard_map/ppermute | solution.py:495

commit v4 on v3

--- a/solution.py
+++ b/solution.py
@@ -204,16 +204,16 @@
             omega = omega_pick[at, :]
             sums = total[...]
             near = []
-            for c in range(0, cols, HALF):
-                square = jnp.dot(rows, src[:, c : c + HALF], preferred_element_type=jnp.float32)
+            for c in range(0, cols, PAIR):
+                square = jnp.dot(rows, src[:, c : c + PAIR], preferred_element_type=jnp.float32)
                 tile = [near_field(square[r : r + PIECE]) for r in range(0, rb, PIECE)]
                 tile = jnp.concatenate(tile, axis=0)
-                sums += jnp.dot(tile, omega[c : c + HALF], preferred_element_type=jnp.float32)
+                sums += jnp.dot(tile, omega[c : c + PAIR], preferred_element_type=jnp.float32)
                 near.append(tile)
             total[...] = sums
             for k in range(GROUP):
-                tile = near[k * WIDTH // HALF]
-                at = k * WIDTH % HALF
+                tile = near[k * WIDTH // PAIR]
+                at = k * WIDTH % PAIR
                 tiles_ref[GROUP * j + k, here, :] = tile[:, at : at + WIDTH]
             return carry
 

time: 86.8 us -> 86.5 us (level)
  the two profiles are of different devices: /device:TPU:3 before, /device:TPU:7 now
where the time goes in v4:
time: 86.5 us; the launch traced here: 86.2 us
  Pallas kernels  38.6 us (45%)
  starting transfers between devices  36.6 us (42%)
  waiting for transfers between devices  10.2 us (12%)
    ppermute x17, starting transfers between devices, swap(): return lax.ppermute(x, 'tile', [(i, i ^ k) for i in range(n)])  36.6 us
    pallas_call x6, Pallas kernels, sketch_pass(): pl.pallas_call(functools.partial(sketch_kernel, first=first, panels=panel...  24.4 us
    ppermute x17, waiting for transfers between devices, swap(): return lax.ppermute(x, 'tile', [(i, i ^ k) for i in range(n)])  10.2 us
    pallas_call x1, Pallas kernels, project_pass(): pl.pallas_call(functools.partial(project_kernel, panels=panels, half=len(...  8.53 us
    pallas_call x1, Pallas kernels, first_pass(): pl.pallas_call(functools.partial(first_kernel, panels=panels, half=len(ev...  2.65 us
    pallas_call x1, Pallas kernels, prep(): pl.pallas_call(functools.partial(prep_kernel, slices=slices, place=place)...  2.63 us
  transfers between devices with their start and end apart: 17, of which 6 were waited for; matrix products, arithmetic and copies ran while one was open for 0% of the time, Pallas kernels for 25%

profile of v4, /device:TPU:7, one launch (start us, length us, event | category | flops | bytes accessed | tf_op | source)
XLA Modules:
  0.0 86.2 jit_solution(7732516416913119672)
XLA Ops:
  0.6 2.6 %prep.1 = (s32[40]{0:T(128)S(1)}, bf16[32,4096]{1,0:T(8,128)(2,1)S(1)}, bf16[4096,128]{1,0:T(8,128)(2,1)S(1)}, bf16[4096,32]{1,0:T(8,128)(2,1)S(1)}) custom-call(s32[1,32]{1,0:T(1,128)} %flags_hbm.1, f32[3,16384]{1,0:T(4,128)} %rows_hbm.1, f32[3,4096]{1,0:T(4,128)} %src_hbm.1, bf16[4096,128]{1,0:T(8,128)(2,1)} %omega_hbm.1), custom_call_target="tpu_custom_call" | custom-call | tf_op jit(solution)/shard_map/prep/pallas_call | solution.py:165
  3.3 5.8 %sketch_pass.6 = (f32[1024,128]{1,0:T(8,128)S(1)}, bf16[32,1024,128]{2,1,0:T(8,128)(2,1)S(1)}) custom-call(s32[40]{0:T(128)S(1)} %get-tuple-element.58.order_ref, bf16[32,4096]{1,0:T(8,128)(2,1)S(1)} %get-tuple-element.40.src_pick, bf16[4096,128]{1,0:T(8,128)(2,1)S(1)} %get-tuple-element.41.omega_pick, bf16[4096,32]{1,0:T(8,128)(2,1)S(1)} %get-tuple-element.42.row_mat), custom_call_target="tpu_custom_call" | custom-call | flops 8589934592 | bytes 8388608 | tf_op jit(solution)/shard_map/sketch_pass/pallas_call | solution.py:231
  9.1 6.0 %collective-permute-start = (f32[1024,128]{1,0:T(8,128)S(1)}, f32[1024,128]{1,0:T(8,128)S(1)}, u32[]{:S(2)}, u32[]{:S(2)}) collective-permute-start(f32[1024,128]{1,0:T(8,128)S(1)} %get-tuple-element.43), channel_id=1, source_target_pairs={{0,1},{1,0},{2,3},{3,2},{4,5},{5,4},{6,7},{7,6},{8,9},{9,8},{10,11... | collective-permute-start | bytes 1572872 | tf_op jit(solution)/shard_map/ppermute | solution.py:495
  15.1 5.8 %sketch_pass.7 = (f32[1024,128]{1,0:T(8,128)S(1)}, bf16[32,1024,128]{2,1,0:T(8,128)(2,1)S(1)}) custom-call(s32[40]{0:T(128)S(1)} %get-tuple-element.58.order_ref, bf16[32,4096]{1,0:T(8,128)(2,1)S(1)} %get-tuple-element.40.src_pick, bf16[4096,128]{1,0:T(8,128)(2,1)S(1)} %get-tuple-element.41.omega_pick, bf16[4096,32]{1,0:T(8,128)(2,1)S(1)} %get-tuple-element.42.row_mat), custom_call_target="tpu_custom_call" | custom-call | flops 8589934592 | bytes 8388608 | tf_op jit(solution)/shard_map/sketch_pass/pallas_call | solution.py:231
  20.9 0.0 collective-permute-done.refs_1_
  20.9 0.1 pair_sum.2
  21.0 1.5 %collective-permute-start.1 = (bf16[256,128]{1,0:T(8,128)(2,1)S(1)}, bf16[256,128]{1,0:T(8,128)(2,1)S(1)}, u32[]{:S(2)}, u32[]{:S(2)}) collective-permute-start(bf16[256,128]{1,0:T(8,128)(2,1)S(1)} %get-tuple-element.52), channel_id=1, source_target_pairs={{0,2},{1,3},{2,0},{3,1},{4,6},{5,7},{6,4},{7,5},{8,10},{9,11},{10,... | collective-permute-start | bytes 196616 | tf_op jit(solution)/shard_map/ppermute | solution.py:495
  22.5 1.2 %collective-permute-start.2 = (bf16[256,128]{1,0:T(8,128)(2,1)S(1)}, bf16[256,128]{1,0:T(8,128)(2,1)S(1)}, u32[]{:S(2)}, u32[]{:S(2)}) collective-permute-start(bf16[256,128]{1,0:T(8,128)(2,1)S(1)} %get-tuple-element.53), channel_id=1, source_target_pairs={{0,4},{1,5},{2,6},{3,7},{4,0},{5,1},{6,2},{7,3},{8,12},{9,13},{10,... | collective-permute-start | bytes 196616 | tf_op jit(solution)/shard_map/ppermute | solution.py:495
  23.7 3.2 %sketch_pass.8 = (f32[512,128]{1,0:T(8,128)S(1)}, bf16[32,512,128]{2,1,0:T(8,128)(2,1)S(1)}) custom-call(s32[40]{0:T(128)S(1)} %get-tuple-element.58.order_ref, bf16[32,4096]{1,0:T(8,128)(2,1)S(1)} %get-tuple-element.40.src_pick, bf16[4096,128]{1,0:T(8,128)(2,1)S(1)} %get-tuple-element.41.omega_pick, bf16[4096,32]{1,0:T(8,128)(2,1)S(1)} %get-tuple-element.42.row_mat), custom_call_target="tpu_custom_call" | custom-call | flops 4294967296 | bytes 4194304 | tf_op jit(solution)/shard_map/sketch_pass/pallas_call | solution.py:231
  26.8 8.1 %collective-permute-start.8 = (f32[512,128]{1,0:T(8,128)S(1)}, f32[512,128]{1,0:T(8,128)S(1)}, u32[]{:S(2)}, u32[]{:S(2)}) collective-permute-start(f32[512,128]{1,0:T(8,128)S(1)} %get-tuple-element.48), channel_id=1, source_target_pairs={{0,1},{1,0},{2,3},{3,2},{4,5},{5,4},{6,7},{7,6},{8,9},{9,8},{10,11... | collective-permute-start | bytes 786440 | tf_op jit(solution)/shard_map/ppermute | solution.py:495
  35.0 0.0 collective-permute-done.1.refs_0_
  35.0 0.0 collective-permute-done.2.refs_1_
  35.0 0.0 collective-permute-start.3
  35.0 3.2 %sketch_pass.9 = (f32[512,128]{1,0:T(8,128)S(1)}, bf16[32,512,128]{2,1,0:T(8,128)(2,1)S(1)}) custom-call(s32[40]{0:T(128)S(1)} %get-tuple-element.58.order_ref, bf16[32,4096]{1,0:T(8,128)(2,1)S(1)} %get-tuple-element.40.src_pick, bf16[4096,128]{1,0:T(8,128)(2,1)S(1)} %get-tuple-element.41.omega_pick, bf16[4096,32]{1,0:T(8,128)(2,1)S(1)} %get-tuple-element.42.row_mat), custom_call_target="tpu_custom_call" | custom-call | flops 4294967296 | bytes 4194304 | tf_op jit(solution)/shard_map/sketch_pass/pallas_call | solution.py:231
  38.2 3.6 %collective-permute-start.9 = (f32[512,128]{1,0:T(8,128)S(1)}, f32[512,128]{1,0:T(8,128)S(1)}, u32[]{:S(2)}, u32[]{:S(2)}) collective-permute-start(f32[512,128]{1,0:T(8,128)S(1)} %get-tuple-element.50), channel_id=1, source_target_pairs={{0,1},{1,0},{2,3},{3,2},{4,5},{5,4},{6,7},{7,6},{8,9},{9,8},{10,11... | collective-permute-start | bytes 786440 | tf_op jit(solution)/shard_map/ppermute | solution.py:495
  41.7 0.0 collective-permute-done.3.refs_2_
  41.7 0.1 row_sum.2.refs_0_
  41.8 2.4 %collective-permute-start.5 = (bf16[128,256]{1,0:T(8,128)(2,1)S(1)}, bf16[128,256]{1,0:T(8,128)(2,1)S(1)}, u32[]{:S(2)}, u32[]{:S(2)}) collective-permute-start(bf16[128,256]{1,0:T(8,128)(2,1)S(1)} %row_sum.2.refs_0_), channel_id=1, source_target_pairs={{0,4},{1,5},{2,6},{3,7},{4,0},{5,1},{6,2},{7,3},{8,12},{9,13},{10,... | collective-permute-start | bytes 196616 | tf_op jit(solution)/shard_map/ppermute | solution.py:495
  44.2 0.0 collective-permute-start.4
  44.2 3.3 %sketch_pass.10 = (f32[512,128]{1,0:T(8,128)S(1)}, bf16[32,512,128]{2,1,0:T(8,128)(2,1)S(1)}) custom-call(s32[40]{0:T(128)S(1)} %get-tuple-element.58.order_ref, bf16[32,4096]{1,0:T(8,128)(2,1)S(1)} %get-tuple-element.40.src_pick, bf16[4096,128]{1,0:T(8,128)(2,1)S(1)} %get-tuple-element.41.omega_pick, bf16[4096,32]{1,0:T(8,128)(2,1)S(1)} %get-tuple-element.42.row_mat), custom_call_target="tpu_custom_call" | custom-call | flops 4294967296 | bytes 4194304 | tf_op jit(solution)/shard_map/sketch_pass/pallas_call | solution.py:231
  47.6 0.0 collective-permute-done.5.refs_2_
  47.6 0.1 collective-permute-done.4.refs_1_
  47.6 1.3 %collective-permute-start.6 = (bf16[128,256]{1,0:T(8,128)(2,1)S(1)}, bf16[128,256]{1,0:T(8,128)(2,1)S(1)}, u32[]{:S(2)}, u32[]{:S(2)}) collective-permute-start(bf16[128,256]{1,0:T(8,128)(2,1)S(1)} %row_sum.2.refs_0_), channel_id=1, source_target_pairs={{0,6},{1,7},{2,4},{3,5},{4,2},{5,3},{6,0},{7,1},{8,14},{9,15},{10,... | collective-permute-start | bytes 196616 | tf_op jit(solution)/shard_map/ppermute | solution.py:495
  48.9 3.2 %sketch_pass.11 = (f32[512,128]{1,0:T(8,128)S(1)}, bf16[32,512,128]{2,1,0:T(8,128)(2,1)S(1)}) custom-call(s32[40]{0:T(128)S(1)} %get-tuple-element.58.order_ref, bf16[32,4096]{1,0:T(8,128)(2,1)S(1)} %get-tuple-element.40.src_pick, bf16[4096,128]{1,0:T(8,128)(2,1)S(1)} %get-tuple-element.41.omega_pick, bf16[4096,32]{1,0:T(8,128)(2,1)S(1)} %get-tuple-element.42.row_mat), custom_call_target="tpu_custom_call" | custom-call | flops 4294967296 | bytes 4194304 | tf_op jit(solution)/shard_map/sketch_pass/pallas_call | solution.py:231
  52.1 0.6 collective-permute-done.6.refs_3_
  52.7 4.1 %collective-permute-start.7 = (bf16[4,128,256]{2,1,0:T(8,128)(2,1)S(1)}, bf16[4,128,256]{2,1,0:T(8,128)(2,1)S(1)}, u32[]{:S(2)}, u32[]{:S(2)}) collective-permute-start(bf16[4,128,256]{2,1,0:T(8,128)(2,1)S(1)} %join.2), channel_id=1, source_target_pairs={{0,1},{1,0},{2,3},{3,2},{4,5},{5,4},{6,7},{7,6},{8,9},{9,8},{10,11... | collective-permute-start | bytes 786440 | tf_op jit(solution)/shard_map/ppermute | solution.py:495
  56.8 0.0 collective-permute-done.8.refs_2_
  56.8 0.0 collective-permute-done.9.refs_3_
  56.8 0.1 pair_sum.3
  56.8 1.8 %collective-permute-start.10 = (bf16[256,128]{1,0:T(8,128)(2,1)S(1)}, bf16[256,128]{1,0:T(8,128)(2,1)S(1)}, u32[]{:S(2)}, u32[]{:S(2)}) collective-permute-start(bf16[256,128]{1,0:T(8,128)(2,1)S(1)} %get-tuple-element.69), channel_id=1, source_target_pairs={{0,2},{1,3},{2,0},{3,1},{4,6},{5,7},{6,4},{7,5},{8,10},{9,11},{10,... | collective-permute-start | bytes 196616 | tf_op jit(solution)/shard_map/ppermute | solution.py:495
  58.6 1.2 %collective-permute-start.11 = (bf16[256,128]{1,0:T(8,128)(2,1)S(1)}, bf16[256,128]{1,0:T(8,128)(2,1)S(1)}, u32[]{:S(2)}, u32[]{:S(2)}) collective-permute-start(bf16[256,128]{1,0:T(8,128)(2,1)S(1)} %get-tuple-element.70), channel_id=1, source_target_pairs={{0,4},{1,5},{2,6},{3,7},{4,0},{5,1},{6,2},{7,3},{8,12},{9,13},{10,... | collective-permute-start | bytes 196616 | tf_op jit(solution)/shard_map/ppermute | solution.py:495
  59.8 1.1 %collective-permute-start.12 = (bf16[256,128]{1,0:T(8,128)(2,1)S(1)}, bf16[256,128]{1,0:T(8,128)(2,1)S(1)}, u32[]{:S(2)}, u32[]{:S(2)}) collective-permute-start(bf16[256,128]{1,0:T(8,128)(2,1)S(1)} %get-tuple-element.71), channel_id=1, source_target_pairs={{0,6},{1,7},{2,4},{3,5},{4,2},{5,3},{6,0},{7,1},{8,14},{9,15},{10,... | collective-permute-start | bytes 196616 | tf_op jit(solution)/shard_map/ppermute | solution.py:495
  60.9 0.0 collective-permute-done.7.odd_ref
  60.9 2.6 %first_pass.1 = (f32[128,4096]{1,0:T(8,128)S(1)}, f32[128,128]{1,0:T(8,128)S(1)}) custom-call(s32[40]{0:T(128)S(1)} %get-tuple-element.58.order_ref, bf16[4,128,256]{2,1,0:T(8,128)(2,1)S(1)} %collective-permute-done.7.odd_ref, bf16[128,256]{1,0:T(8,128)(2,1)S(1)} %row_sum.2.refs_0_, bf16[128,256]{1,0:T(8,128)(2,1)S(1)} %collective-permute-done.4.refs_1_, ...), custom_call_target="tpu_custom_call" | custom-call | flops 2147483648 | tf_op jit(solution)/shard_map/first_pass/pallas_call | solution.py:383
  63.6 0.0 collective-permute-done.10.refs_0_
  63.6 0.0 collective-permute-done.11.refs_1_
  63.6 2.4 %collective-permute-done.12.refs_2_ = bf16[256,128]{1,0:T(8,128)(2,1)S(1)} collective-permute-done((bf16[256,128]{1,0:T(8,128)(2,1)S(1)}, bf16[256,128]{1,0:T(8,128)(2,1)S(1)}, u32[]{:S(2)}, u32[]{:S(2)}) %collective-permute-start.12) | collective-permute-done | bytes 65568 | tf_op jit(solution)/shard_map/ppermute | solution.py:495
  66.0 0.1 row_sum.3.refs_0_.refs_1_.refs_2_
  66.1 2.4 %collective-permute-start.15 = (bf16[128,256]{1,0:T(8,128)(2,1)S(1)}, bf16[128,256]{1,0:T(8,128)(2,1)S(1)}, u32[]{:S(2)}, u32[]{:S(2)}) collective-permute-start(bf16[128,256]{1,0:T(8,128)(2,1)S(1)} %row_sum.3.refs_0_.refs_1_.refs_2_), channel_id=1, source_target_pairs={{0,6},{1,7},{2,4},{3,5},{4,2},{5,3},{6,0},{7,1},{8,14},{9,15},{10,... | collective-permute-start | bytes 196616 | tf_op jit(solution)/shard_map/ppermute | solution.py:495
  68.5 0.6 collective-permute-start.14
  69.2 0.5 collective-permute-start.13
  69.7 1.5 %collective-permute-done.15.refs_3_.refs_5_ = bf16[128,256]{1,0:T(8,128)(2,1)S(1)} collective-permute-done((bf16[128,256]{1,0:T(8,128)(2,1)S(1)}, bf16[128,256]{1,0:T(8,128)(2,1)S(1)}, u32[]{:S(2)}, u32[]{:S(2)}) %collective-permute-start.15) | collective-permute-done | bytes 65568 | tf_op jit(solution)/shard_map/ppermute | solution.py:495
  71.2 4.5 %collective-permute-done.14.refs_2_.refs_4_ = bf16[128,256]{1,0:T(8,128)(2,1)S(1)} collective-permute-done((bf16[128,256]{1,0:T(8,128)(2,1)S(1)}, bf16[128,256]{1,0:T(8,128)(2,1)S(1)}, u32[]{:S(2)}, u32[]{:S(2)}) %collective-permute-start.14) | collective-permute-done | bytes 65568 | tf_op jit(solution)/shard_map/ppermute | solution.py:495
  75.7 0.0 collective-permute-done.13.refs_1_.refs_3_
  75.7 0.8 collective-permute-start.16
  76.5 1.2 %collective-permute-done.16.odd_ref = bf16[4,128,256]{2,1,0:T(8,128)(2,1)S(1)} collective-permute-done((bf16[4,128,256]{2,1,0:T(8,128)(2,1)S(1)}, bf16[4,128,256]{2,1,0:T(8,128)(2,1)S(1)}, u32[]{:S(2)}, u32[]{:S(2)}) %collective-permute-start.16) | collective-permute-done | bytes 262176 | tf_op jit(solution)/shard_map/ppermute | solution.py:495
  77.7 8.5 %project_pass.1 = (f32[512,128]{1,0:T(8,128)}, bf16[1,128,4096]{2,1,0:T(8,128)(2,1)}) custom-call(s32[40]{0:T(128)S(1)} %get-tuple-element.58.order_ref, f32[128,4096]{1,0:T(8,128)S(1)} %get-tuple-element.64.first_ref, f32[128,128]{1,0:T(8,128)S(1)} %get-tuple-element.65.gram_ref, bf16[4,128,256]{2,1,0:T(8,128)(2,1)S(1)} %collective-permute-done.16.odd_ref, ...), custom_call_target="tpu_custom_call" | custom-call | tf_op jit(solution)/shard_map/project_pass/pallas_call | solution.py:457
  (2 shorter events, 0.0 us)
Async XLA Ops:
  9.1 11.9 %collective-permute-start = (f32[1024,128]{1,0:T(8,128)S(1)}, f32[1024,128]{1,0:T(8,128)S(1)}, u32[]{:S(2)}, u32[]{:S(2)}) collective-permute-start(f32[1024,128]{1,0:T(8,128)S(1)} %get-tuple-element.43), channel_id=1, source_target_pairs={{0,1},{1,0},{2,3},{3,2},{4,5},{5,4},{6,7},{7,6},{8,9},{9,8},{10,11... | collective-permute-start | bytes 1572872 | tf_op jit(solution)/shard_map/ppermute | solution.py:495
  21.0 14.0 %collective-permute-start.1 = (bf16[256,128]{1,0:T(8,128)(2,1)S(1)}, bf16[256,128]{1,0:T(8,128)(2,1)S(1)}, u32[]{:S(2)}, u32[]{:S(2)}) collective-permute-start(bf16[256,128]{1,0:T(8,128)(2,1)S(1)} %get-tuple-element.52), channel_id=1, source_target_pairs={{0,2},{1,3},{2,0},{3,1},{4,6},{5,7},{6,4},{7,5},{8,10},{9,11},{10,... | collective-permute-start | bytes 196616 | tf_op jit(solution)/shard_map/ppermute | solution.py:495
  22.5 12.5 %collective-permute-start.2 = (bf16[256,128]{1,0:T(8,128)(2,1)S(1)}, bf16[256,128]{1,0:T(8,128)(2,1)S(1)}, u32[]{:S(2)}, u32[]{:S(2)}) collective-permute-start(bf16[256,128]{1,0:T(8,128)(2,1)S(1)} %get-tuple-element.53), channel_id=1, source_target_pairs={{0,4},{1,5},{2,6},{3,7},{4,0},{5,1},{6,2},{7,3},{8,12},{9,13},{10,... | collective-permute-start | bytes 196616 | tf_op jit(solution)/shard_map/ppermute | solution.py:495
  26.8 30.0 %collective-permute-start.8 = (f32[512,128]{1,0:T(8,128)S(1)}, f32[512,128]{1,0:T(8,128)S(1)}, u32[]{:S(2)}, u32[]{:S(2)}) collective-permute-start(f32[512,128]{1,0:T(8,128)S(1)} %get-tuple-element.48), channel_id=1, source_target_pairs={{0,1},{1,0},{2,3},{3,2},{4,5},{5,4},{6,7},{7,6},{8,9},{9,8},{10,11... | collective-permute-start | bytes 786440 | tf_op jit(solution)/shard_map/ppermute | solution.py:495
  35.0 6.8 %collective-permute-start.3 = (bf16[256,128]{1,0:T(8,128)(2,1)S(1)}, bf16[256,128]{1,0:T(8,128)(2,1)S(1)}, u32[]{:S(2)}, u32[]{:S(2)}) collective-permute-start(bf16[256,128]{1,0:T(8,128)(2,1)S(1)} %get-tuple-element.55), channel_id=1, source_target_pairs={{0,6},{1,7},{2,4},{3,5},{4,2},{5,3},{6,0},{7,1},{8,14},{9,15},{10,... | collective-permute-start | bytes 196616 | tf_op jit(solution)/shard_map/ppermute | solution.py:495
  38.2 18.6 %collective-permute-start.9 = (f32[512,128]{1,0:T(8,128)S(1)}, f32[512,128]{1,0:T(8,128)S(1)}, u32[]{:S(2)}, u32[]{:S(2)}) collective-permute-start(f32[512,128]{1,0:T(8,128)S(1)} %get-tuple-element.50), channel_id=1, source_target_pairs={{0,1},{1,0},{2,3},{3,2},{4,5},{5,4},{6,7},{7,6},{8,9},{9,8},{10,11... | collective-permute-start | bytes 786440 | tf_op jit(solution)/shard_map/ppermute | solution.py:495
  41.8 5.7 %collective-permute-start.5 = (bf16[128,256]{1,0:T(8,128)(2,1)S(1)}, bf16[128,256]{1,0:T(8,128)(2,1)S(1)}, u32[]{:S(2)}, u32[]{:S(2)}) collective-permute-start(bf16[128,256]{1,0:T(8,128)(2,1)S(1)} %row_sum.2.refs_0_), channel_id=1, source_target_pairs={{0,4},{1,5},{2,6},{3,7},{4,0},{5,1},{6,2},{7,3},{8,12},{9,13},{10,... | collective-permute-start | bytes 196616 | tf_op jit(solution)/shard_map/ppermute | solution.py:495
  44.2 3.4 %collective-permute-start.4 = (bf16[128,256]{1,0:T(8,128)(2,1)S(1)}, bf16[128,256]{1,0:T(8,128)(2,1)S(1)}, u32[]{:S(2)}, u32[]{:S(2)}) collective-permute-start(bf16[128,256]{1,0:T(8,128)(2,1)S(1)} %row_sum.2.refs_0_), channel_id=1, source_target_pairs={{0,2},{1,3},{2,0},{3,1},{4,6},{5,7},{6,4},{7,5},{8,10},{9,11},{10,... | collective-permute-start | bytes 196616 | tf_op jit(solution)/shard_map/ppermute | solution.py:495
  47.6 5.0 %collective-permute-start.6 = (bf16[128,256]{1,0:T(8,128)(2,1)S(1)}, bf16[128,256]{1,0:T(8,128)(2,1)S(1)}, u32[]{:S(2)}, u32[]{:S(2)}) collective-permute-start(bf16[128,256]{1,0:T(8,128)(2,1)S(1)} %row_sum.2.refs_0_), channel_id=1, source_target_pairs={{0,6},{1,7},{2,4},{3,5},{4,2},{5,3},{6,0},{7,1},{8,14},{9,15},{10,... | collective-permute-start | bytes 196616 | tf_op jit(solution)/shard_map/ppermute | solution.py:495
  52.7 8.2 %collective-permute-start.7 = (bf16[4,128,256]{2,1,0:T(8,128)(2,1)S(1)}, bf16[4,128,256]{2,1,0:T(8,128)(2,1)S(1)}, u32[]{:S(2)}, u32[]{:S(2)}) collective-permute-start(bf16[4,128,256]{2,1,0:T(8,128)(2,1)S(1)} %join.2), channel_id=1, source_target_pairs={{0,1},{1,0},{2,3},{3,2},{4,5},{5,4},{6,7},{7,6},{8,9},{9,8},{10,11... | collective-permute-start | bytes 786440 | tf_op jit(solution)/shard_map/ppermute | solution.py:495
  56.8 6.7 %collective-permute-start.10 = (bf16[256,128]{1,0:T(8,128)(2,1)S(1)}, bf16[256,128]{1,0:T(8,128)(2,1)S(1)}, u32[]{:S(2)}, u32[]{:S(2)}) collective-permute-start(bf16[256,128]{1,0:T(8,128)(2,1)S(1)} %get-tuple-element.69), channel_id=1, source_target_pairs={{0,2},{1,3},{2,0},{3,1},{4,6},{5,7},{6,4},{7,5},{8,10},{9,11},{10,... | collective-permute-start | bytes 196616 | tf_op jit(solution)/shard_map/ppermute | solution.py:495
  58.6 5.0 %collective-permute-start.11 = (bf16[256,128]{1,0:T(8,128)(2,1)S(1)}, bf16[256,128]{1,0:T(8,128)(2,1)S(1)}, u32[]{:S(2)}, u32[]{:S(2)}) collective-permute-start(bf16[256,128]{1,0:T(8,128)(2,1)S(1)} %get-tuple-element.70), channel_id=1, source_target_pairs={{0,4},{1,5},{2,6},{3,7},{4,0},{5,1},{6,2},{7,3},{8,12},{9,13},{10,... | collective-permute-start | bytes 196616 | tf_op jit(solution)/shard_map/ppermute | solution.py:495
  59.8 6.2 %collective-permute-start.12 = (bf16[256,128]{1,0:T(8,128)(2,1)S(1)}, bf16[256,128]{1,0:T(8,128)(2,1)S(1)}, u32[]{:S(2)}, u32[]{:S(2)}) collective-permute-start(bf16[256,128]{1,0:T(8,128)(2,1)S(1)} %get-tuple-element.71), channel_id=1, source_target_pairs={{0,6},{1,7},{2,4},{3,5},{4,2},{5,3},{6,0},{7,1},{8,14},{9,15},{10,... | collective-permute-start | bytes 196616 | tf_op jit(solution)/shard_map/ppermute | solution.py:495
  66.1 5.1 %collective-permute-start.15 = (bf16[128,256]{1,0:T(8,128)(2,1)S(1)}, bf16[128,256]{1,0:T(8,128)(2,1)S(1)}, u32[]{:S(2)}, u32[]{:S(2)}) collective-permute-start(bf16[128,256]{1,0:T(8,128)(2,1)S(1)} %row_sum.3.refs_0_.refs_1_.refs_2_), channel_id=1, source_target_pairs={{0,6},{1,7},{2,4},{3,5},{4,2},{5,3},{6,0},{7,1},{8,14},{9,15},{10,... | collective-permute-start | bytes 196616 | tf_op jit(solution)/shard_map/ppermute | solution.py:495
  68.5 7.1 %collective-permute-start.14 = (bf16[128,256]{1,0:T(8,128)(2,1)S(1)}, bf16[128,256]{1,0:T(8,128)(2,1)S(1)}, u32[]{:S(2)}, u32[]{:S(2)}) collective-permute-start(bf16[128,256]{1,0:T(8,128)(2,1)S(1)} %row_sum.3.refs_0_.refs_1_.refs_2_), channel_id=1, source_target_pairs={{0,4},{1,5},{2,6},{3,7},{4,0},{5,1},{6,2},{7,3},{8,12},{9,13},{10,... | collective-permute-start | bytes 196616 | tf_op jit(solution)/shard_map/ppermute | solution.py:495
  69.2 6.5 %collective-permute-start.13 = (bf16[128,256]{1,0:T(8,128)(2,1)S(1)}, bf16[128,256]{1,0:T(8,128)(2,1)S(1)}, u32[]{:S(2)}, u32[]{:S(2)}) collective-permute-start(bf16[128,256]{1,0:T(8,128)(2,1)S(1)} %row_sum.3.refs_0_.refs_1_.refs_2_), channel_id=1, source_target_pairs={{0,2},{1,3},{2,0},{3,1},{4,6},{5,7},{6,4},{7,5},{8,10},{9,11},{10,... | collective-permute-start | bytes 196616 | tf_op jit(solution)/shard_map/ppermute | solution.py:495
  75.7 2.0 %collective-permute-start.16 = (bf16[4,128,256]{2,1,0:T(8,128)(2,1)S(1)}, bf16[4,128,256]{2,1,0:T(8,128)(2,1)S(1)}, u32[]{:S(2)}, u32[]{:S(2)}) collective-permute-start(bf16[4,128,256]{2,1,0:T(8,128)(2,1)S(1)} %join.3), channel_id=1, source_target_pairs={{0,1},{1,0},{2,3},{3,2},{4,5},{5,4},{6,7},{7,6},{8,9},{9,8},{10,11... | collective-permute-start | bytes 786440 | tf_op jit(solution)/shard_map/ppermute | solution.py:495
